TPU v7x, 256 devices: a whole 4x4x8 slice. The times are simulated.
256 devices in a mesh: group: 2 (over core), seq: 16 (over y, x), head: 8 (over z).
Axes of the slice: x: 4, y: 4, z: 8, core: 2. Of those that a mesh axis runs over, the one named last changes fastest.
Arguments:
- x_in: bfloat16 [24576, 8192], P(('group', 'seq'), 'head'), parts along dimension 0, may hold values from -6 to 6
- bc_in: bfloat16 [24576, 8, 512], P(('group', 'seq'), 'head'), parts along dimension 0, may hold values from -6 to 6
- dt_in: float32 [24576, 128], P(('group', 'seq'), 'head'), parts along dimension 0, may hold values from -5 to 5
- conv_x: float32 [4, 8192], P(None, 'head'), may hold values from -3 to 3
- conv_bc: float32 [4, 8, 512], P(None, 'head'), may hold values from -3 to 3
- a_log: float32 [128], P('head'), may hold values from -11 to -2.5
- dt_bias: float32 [128], P('head'), may hold values from -1 to 1
- d_skip: float32 [128], P('head'), may hold values from 0.5 to 1.5
- norm_gain: float32 [8192], P('head'), may hold values from 0.5 to 1.5
- doc_lengths: int32 [16], P('group'), parts along dimension 0, may hold values from 1 to 9216, 12288 in all
- dec_x: bfloat16 [32, 8, 8192], P(('group', 'seq'), None, 'head'), parts along dimension 0, may hold values from -6 to 6
- dec_bc: bfloat16 [32, 8, 8, 512], P(('group', 'seq'), None, 'head'), parts along dimension 0, may hold values from -6 to 6
- dec_dt: float32 [32, 8, 128], P(('group', 'seq'), None, 'head'), parts along dimension 0, may hold values from -5 to 5
Outputs:
- prompt_out: bfloat16 [24576, 8192], P(('group', 'seq'), 'head'), parts along dimension 0
- decode_out: bfloat16 [32, 8, 8192], P(('group', 'seq'), None, 'head'), parts along dimension 0
There are 2 independent parts, one for each index of `group`. A program takes and returns all parts, laid end to end along the dimension named above; an argument that names none is the same for every part. Nothing has to cross between parts.
Inputs may be any that keep to these rules, and one draw needn't show every extreme that they name: `doc_lengths`: the samples continue the last of the 8 documents.
All inputs are finite; a program needn't handle non-finite values.
Results may differ from a plain program's by a relative error of at most 0.0035.
Values may be sent and summed in bfloat16 or wider, within the bound.
A program may use at most 128 MiB of HBM per device.

v0:
```python
import jax
import jax.numpy as jnp
from jax import lax
from jax.sharding import PartitionSpec as P

CONV = 4
BLOCK = 256


epsilon = 1e-05


def shifted(block, axis, distance):
    devices = range(lax.axis_size(axis))
    route = [(i - distance, i) for i in devices if i - distance in devices]
    return lax.ppermute(block, axis, route)


def entering(value, axis, combine, identity):
    length, index = (lax.axis_size(axis), lax.axis_index(axis))
    everything = jax.tree.map(lambda part: lax.all_gather(part, axis), value)
    start = jax.tree.map(
        lambda part, zero: jnp.broadcast_to(jnp.asarray(zero, part.dtype), part.shape),
        value,
        identity,
    )

    def step(k, before):
        reached = k < index
        new = combine(before, jax.tree.map(lambda part: part[k], everything))
        return jax.tree.map(lambda a, b: jnp.where(reached, a, b), new, before)

    return lax.fori_loop(0, length, step, start)


def from_root(value, axis, root):
    mine = lax.axis_index(axis) == root
    return lax.psum(jnp.where(mine, value, jnp.zeros_like(value)), axis)


def seg_of(doc_lengths, positions):
    doc_ends = jnp.cumsum(doc_lengths)
    counted = jnp.sum((positions[:, None] >= doc_ends[None, :]).astype(jnp.int32), axis=1)
    return jnp.where(positions < 0, jnp.int32(-1), counted)


def conv_silu(extended, ext_seg, taps):
    tok_count = extended.shape[0] - CONV + 1
    mine_seg = ext_seg[CONV - 1 :]
    totals = jnp.zeros((tok_count,) + extended.shape[1:], jnp.float32)
    for tap_index in range(CONV):
        same_doc = (ext_seg[tap_index : tap_index + tok_count] == mine_seg).astype(jnp.float32)
        same_doc = same_doc.reshape((tok_count,) + (1,) * (extended.ndim - 1))
        totals = (
            totals
            + taps[tap_index]
            * extended[tap_index : tap_index + tok_count].astype(jnp.float32)
            * same_doc
        )
    return jax.nn.silu(totals).astype(jnp.bfloat16)


def block_terms(x_block, bc_block, dt_block, linear_attention_block, seg_block, seg_before, d_skip):
    tok_count, heads_here, head_width = x_block.shape
    groups_here = bc_block.shape[1]
    per_group = heads_here // groups_here
    state_size = bc_block.shape[2] // 2
    b_part = bc_block[:, :, :state_size]
    readout_part = bc_block[:, :, state_size:]
    input_split = x_block.reshape(tok_count, groups_here, per_group, head_width)
    cumul = jnp.cumsum(linear_attention_block, axis=0)
    positions_in = jnp.arange(tok_count)
    allowed = (positions_in[:, None] >= positions_in[None, :]) & (
        seg_block[:, None] == seg_block[None, :]
    )
    scores = jnp.einsum("tgn,sgn->gts", readout_part, b_part, preferred_element_type=jnp.float32)
    cumul_split = cumul.T.reshape(groups_here, per_group, tok_count)
    cum_gaps = cumul_split[:, :, :, None] - cumul_split[:, :, None, :]
    decay_factors = jnp.exp(jnp.where(allowed[None, None], cum_gaps, -jnp.inf))
    dt_split = dt_block.T.reshape(groups_here, per_group, tok_count)
    mixing_matrix = (scores[:, None] * decay_factors * dt_split[:, :, None, :]).astype(jnp.bfloat16)
    inner_piece = jnp.einsum(
        "kaew,wkal->ekal", mixing_matrix, input_split, preferred_element_type=jnp.float32
    )
    last_cum = cumul[-1]
    same_end = (seg_block == seg_block[-1]).astype(jnp.float32)
    inflow_scale = jnp.exp(last_cum[None, :] - cumul) * same_end[:, None] * dt_block
    inflow = (
        b_part[:, :, None, :].astype(jnp.float32)
        * inflow_scale.reshape(tok_count, groups_here, per_group)[:, :, :, None]
    ).astype(jnp.bfloat16)
    block_state = jnp.einsum(
        "sgrp,sgrn->grpn", input_split, inflow, preferred_element_type=jnp.float32
    ).reshape(heads_here, head_width, state_size)
    through = jnp.exp(last_cum) * (seg_block[-1] == seg_before).astype(jnp.float32)
    keep_factor = jnp.exp(cumul) * (seg_block == seg_before).astype(jnp.float32)[:, None]
    local_part = inner_piece.reshape(tok_count, heads_here, head_width) + d_skip[
        None, :, None
    ] * x_block.astype(jnp.float32)
    return (local_part, keep_factor, through, block_state)


def carried_part(bc_block, state_in, keep_factor):
    tok_count, groups_here, doubled = bc_block.shape
    state_size = doubled // 2
    heads_here, head_width, state_dim = state_in.shape
    readout_part = bc_block[:, :, state_size:]
    rounded = state_in.astype(jnp.bfloat16).reshape(
        groups_here, heads_here // groups_here, head_width, state_dim
    )
    result = jnp.einsum(
        "tgn,grpn->tgrp", readout_part, rounded, preferred_element_type=jnp.float32
    ).reshape(tok_count, heads_here, head_width)
    return result * keep_factor[:, :, None]


def group_norm(raw_out, norm_gain, groups_here):
    tok_count = raw_out.shape[0]
    grouped = raw_out.reshape(tok_count, groups_here, -1)
    scaling = lax.rsqrt(jnp.mean(grouped * grouped, axis=-1, keepdims=True) + epsilon)
    return ((grouped * scaling).reshape(tok_count, -1) * norm_gain).astype(jnp.bfloat16)


def decode_one(
    tail_x,
    tail_bc,
    tail_seg,
    last_seg,
    dec_x,
    dec_bc,
    dec_dt,
    start_state,
    conv_x,
    conv_bc,
    a_log,
    dt_bias,
    d_skip,
    norm_gain,
):
    step_count = dec_x.shape[0]
    ext_seg = jnp.concatenate([tail_seg, jnp.full((step_count,), last_seg, jnp.int32)])
    x_steps = conv_silu(jnp.concatenate([tail_x, dec_x]), ext_seg, conv_x)
    bc_steps = conv_silu(jnp.concatenate([tail_bc, dec_bc]), ext_seg, conv_bc)
    heads_here, head_width, state_size = start_state.shape
    groups_here = bc_steps.shape[1]
    per_group = heads_here // groups_here
    step_dt = jax.nn.softplus(dec_dt + dt_bias)
    step_decay = jnp.exp(-step_dt * jnp.exp(a_log))
    current = start_state.reshape(groups_here, per_group, head_width, state_size)
    outputs = []
    for step_index in range(step_count):
        x_now = x_steps[step_index].astype(jnp.float32).reshape(groups_here, per_group, head_width)
        b_now = bc_steps[step_index, :, :state_size].astype(jnp.float32)
        c_now = bc_steps[step_index, :, state_size:].astype(jnp.float32)
        decay_now = step_decay[step_index].reshape(groups_here, per_group)
        dt_now = step_dt[step_index].reshape(groups_here, per_group)
        current = (
            decay_now[:, :, None, None] * current
            + (dt_now[:, :, None] * x_now)[:, :, :, None] * b_now[:, None, None, :]
        )
        reading = jnp.einsum("grpn,gn->grp", current, c_now, precision=lax.Precision.HIGHEST)
        reading = reading + d_skip.reshape(groups_here, per_group)[:, :, None] * x_now
        outputs.append(reading.reshape(heads_here, head_width))
    return group_norm(jnp.stack(outputs), norm_gain, groups_here)


def combine(earlier, later):
    return (earlier[0] * later[0], later[0][:, None, None] * earlier[1] + later[1])


def body(
    x_in,
    bc_in,
    dt_in,
    conv_x,
    conv_bc,
    a_log,
    dt_bias,
    d_skip,
    norm_gain,
    doc_lengths,
    dec_x,
    dec_bc,
    dec_dt,
):
    tok_rows, inner_here = x_in.shape
    heads_here = dt_in.shape[1]
    groups_here = bc_in.shape[1]
    doubled = bc_in.shape[2]
    state_size = doubled // 2
    head_width = inner_here // heads_here
    seq_count = lax.axis_size("seq")
    seq_rank = lax.axis_index("seq")
    reach = CONV - 1
    tok_total = tok_rows * seq_count
    rim_rows = jnp.concatenate(
        [x_in[tok_rows - reach :], bc_in[tok_rows - reach :].reshape(reach, groups_here * doubled)],
        axis=1,
    )
    rim_back = shifted(rim_rows, "seq", 1)
    rim_x = rim_back[:, :inner_here]
    rim_bc = rim_back[:, inner_here:].reshape(reach, groups_here, doubled)
    ext_pos = seq_rank * tok_rows - reach + jnp.arange(tok_rows + reach, dtype=jnp.int32)
    ext_seg = seg_of(doc_lengths, ext_pos)
    x_conv = conv_silu(jnp.concatenate([rim_x, x_in]), ext_seg, conv_x)
    bc_conv = conv_silu(jnp.concatenate([rim_bc, bc_in]), ext_seg, conv_bc)
    step_dt = jax.nn.softplus(dt_in + dt_bias)
    log_decay = -step_dt * jnp.exp(a_log)
    tok_seg = ext_seg[reach:]
    block_count = tok_rows // BLOCK
    before_seg = ext_seg[reach - 1 + jnp.arange(block_count) * BLOCK]
    x_blocks = x_conv.reshape(block_count, BLOCK, heads_here, head_width)
    bc_blocks = bc_conv.reshape(block_count, BLOCK, groups_here, doubled)
    blocks = (
        x_blocks,
        bc_blocks,
        step_dt.reshape(block_count, BLOCK, heads_here),
        log_decay.reshape(block_count, BLOCK, heads_here),
        tok_seg.reshape(block_count, BLOCK),
        before_seg,
    )

    def local_block(block):
        x_block, bc_block, dt_block, linear_attention_block, seg_block, seg_before = block
        return block_terms(
            x_block, bc_block, dt_block, linear_attention_block, seg_block, seg_before, d_skip
        )

    local_parts, keep_factors, throughs, block_states = lax.map(local_block, blocks)

    def summarize(carry, piece):
        return (combine(carry, piece), None)

    empty_state = jnp.zeros((heads_here, head_width, state_size), jnp.float32)
    unit_decay = jnp.ones((heads_here,), jnp.float32)
    summary, unused = lax.scan(summarize, (unit_decay, empty_state), (throughs, block_states))
    tail_x = x_in[tok_rows - reach :]
    tail_bc = bc_in[tok_rows - reach :]
    before_all = entering(summary, "seq", combine, (unit_decay, empty_state))
    state_enter = before_all[1]

    def advance(state_in, block):
        local_part, keep_factor, through, block_state, bc_block = block
        result = local_part + carried_part(bc_block, state_in, keep_factor)
        return (through[:, None, None] * state_in + block_state, result)

    state_after, raw_blocks = lax.scan(
        advance, state_enter, (local_parts, keep_factors, throughs, block_states, bc_blocks)
    )
    prompt_out = group_norm(
        raw_blocks.reshape(tok_rows, heads_here, head_width), norm_gain, groups_here
    )
    state_numel = heads_here * head_width * state_size
    tail_numel = reach * inner_here
    packed = jnp.concatenate(
        [
            state_after.reshape(-1),
            tail_x.astype(jnp.float32).reshape(-1),
            tail_bc.astype(jnp.float32).reshape(-1),
        ]
    )
    arrived = from_root(packed, "seq", seq_count - 1)
    final_state = arrived[:state_numel].reshape(heads_here, head_width, state_size)
    final_input = (
        arrived[state_numel : state_numel + tail_numel]
        .reshape(reach, inner_here)
        .astype(jnp.bfloat16)
    )
    last_bc = (
        arrived[state_numel + tail_numel :]
        .reshape(reach, groups_here, doubled)
        .astype(jnp.bfloat16)
    )
    tail_pos = tok_total - reach + jnp.arange(reach, dtype=jnp.int32)
    tail_seg = seg_of(doc_lengths, tail_pos)
    last_seg = doc_lengths.shape[0] - 1

    def sample(one_x, one_bc, one_dt):
        return decode_one(
            final_input,
            last_bc,
            tail_seg,
            last_seg,
            one_x,
            one_bc,
            one_dt,
            final_state,
            conv_x,
            conv_bc,
            a_log,
            dt_bias,
            d_skip,
            norm_gain,
        )

    decode_out = jax.vmap(sample)(dec_x, dec_bc, dec_dt)
    return (prompt_out, decode_out)


def solution(mesh):
    placed = (
        P(("group", "seq"), "head"),
        P(("group", "seq"), "head", None),
        P(("group", "seq"), "head"),
        P(None, "head"),
        P(None, "head", None),
        P("head"),
        P("head"),
        P("head"),
        P("head"),
        P("group"),
        P(("group", "seq"), None, "head"),
        P(("group", "seq"), None, "head", None),
        P(("group", "seq"), None, "head"),
    )
    return jax.shard_map(
        body,
        mesh=mesh,
        in_specs=placed,
        out_specs=(P(("group", "seq"), "head"), P(("group", "seq"), None, "head")),
        check_vma=False,
    )
```

profile of v0, /device:TPU:32, one launch (start us, length us, event | category | flops | bytes accessed | tf_op | source)
XLA Modules:
  0.0 396.1 jit_solution(15609898351334947949)
XLA Ops:
  9.2 3.4 collective-permute-start
  19.9 6.7 %multiply_convert_fusion.15 = bf16[768,1024]{1,0:T(8,128)(2,1)S(1)} fusion(bf16[768,1024]{1,0:T(8,128)(2,1)} %param.21, bf16[3,1024]{1,0:T(4,128)(2,1)S(1)} %slice.356, f32[1024]{0:T(1024)S(1)} %bitcast.367, f32[768]{0:T(1024)S(1)} %get-tuple-element.520, f32[1024]{0:T(1024)S(1)} %bitcast.369, f32[768]{0:T(1024)S(1)} %get-tuple-element.521, ...), kind=kLoop, calls=%fused_computation.69 | loop fusion | flops 22020096 | bytes 3177472 | tf_op jit(solution)/shard_map/convert_element_type | solution.py:60
  26.5 3.3 reshape.1891
  29.9 5.0 %copy.54 = bf16[3,256,16,64]{1,3,2,0:T(8,128)(2,1)} copy(bf16[3,256,16,64]{3,2,1,0:T(8,128)(2,1)} %reshape.1891) | data formatting | bytes 3145728 | tf_op jit(solution)/shard_map/while | solution.py:229
  35.0 2.2 multiply_convert_fusion.16
  39.3 39.4 %while.55 = (s32[]{:T(128)}, f32[3,256,16,64]{1,3,2,0:T(8,128)}, f32[3,256,16]{1,2,0:T(8,128)S(1)}, f32[3,16]{1,0:T(4,128)S(1)}, f32[3,16,64,256]{3,2,1,0:T(8,12...) while((s32[]{:T(128)}, f32[3,256,16,64]{1,3,2,0:T(8,128)}, ...), condition=%wide.region_5.6_spmd, body=%wide.region_2.5_spmd.sunk | while | flops 310928448 | bytes 6141239 | solution.py:229
  41.3 3.5 fusion.91
  49.7 2.8 fusion.93
  54.5 3.6 fusion.91
  62.8 2.8 fusion.93
  67.6 3.6 fusion.91
  76.0 2.8 fusion.93
  78.8 4.4 %while.57 = (s32[]{:T(128)}, f32[16]{0:T(128)S(1)}, f32[16,64,256]{2,1,0:T(8,128)S(1)}, f32[3,16]{1,0:T(4,128)S(1)}, f32[3,16,64,256]{3,2,1,0:T(8,128)}, /*index=5*/s32[]{:T(128)}, s32[]{:T(128)}) while((s32[]{:T(128)}, f32[16]{0:T(128)S(1)}, f32[16,64,256]{2,1,0:T(8,128)S(1)}, f32[3,16]{1,0:T(4,128)S(1)}, ...), condition=%wide.region_7.8_spmd.clone, body=%wide.region_6.7_spmd.clone.sunk | while | flops 786467 | bytes 3146152 | solution.py:236
  99.8 39.0 %all-reduce.1 = f32[256]{0:T(256)S(1)} all-reduce(f32[256]{0:T(256)S(1)} %dynamic-update-slice), channel_id=2, replica_groups=mesh['group'=2,'seq'=16,'head'=8] {'seq'}, use_global_device_ids=true, to_apply=%add.1 | all-reduce | flops 256 | bytes 2048
  138.8 64.4 %all-gather.4.cloned.1.call-done = f32[256,64,256]{2,1,0:T(8,128)} async-done(((f32[16,64,256]{2,1,0:T(8,128)}), f32[256,64,256]{2,1,0:T(8,128)}) %all-gather.4.cloned.1.call-update) | async-done | bytes 16777232 | tf_op jit(solution)/shard_map/all_gather | solution.py:21
  203.2 24.0 %while.58 = (s32[]{:T(128)}, f32[16,64,256]{2,1,0:T(8,128)S(1)}, s32[]{:T(128)}, f32[16,16]{1,0:T(8,128)S(1)}, f32[16,16,64,256]{3,2,1,0:T(8,128)}, /*index=5*/s32[]{:T(128)}, s32[]{:T(128)}) while((s32[]{:T(128)}, f32[16,64,256]{2,1,0:T(8,128)S(1)}, s32[]{:T(128)}, f32[16,16]{1,0:T(8,128)S(1)}, f32[16,16,64,256]{3,2,1,0:T(8,128)}, ...), condition=%wide.region_9.10_spmd.clone, body=%wide.region_8.9_spmd.clone.sunk | while | flops 1048580 | bytes 3146033 | solution.py:33
  229.2 12.3 %while.56 = (s32[]{:T(128)}, f32[16,64,256]{2,1,0:T(8,128)S(1)}, f32[3,256,16,64]{1,3,2,0:T(8,128)}, f32[3,16]{1,0:T(4,128)S(1)}, f32[3,16,64,256]{3,2,1,0:T(8,1...) while((s32[]{:T(128)}, f32[16,64,256]{2,1,0:T(8,128)S(1)}, ...), condition=%wide.region_11.12_spmd, body=%wide.region_10.11_spmd.sunk | while | flops 135528448 | bytes 6996281 | solution.py:247
  229.3 2.5 fusion.96
  233.3 2.6 fusion.96
  237.5 2.5 fusion.96
  246.5 2.4 copy.79
  249.6 2.2 multiply_convert_fusion.14
  253.5 86.4 %all-reduce.4.cloned.1.call-done = f32[266752]{0:T(1024)} async-done(((f32[266752]{0:T(1024)}), f32[266752]{0:T(1024)}) %all-reduce.4.cloned.1.call-update) | async-done | bytes 1067024 | tf_op jit(solution)/shard_map/psum | solution.py:38
  356.9 8.9 %multiply_add_fusion = (f32[262144]{0:T(1024)}, f32[262144]{0:T(1024)}, f32[262144]{0:T(1024)}, f32[262144]{0:T(1024)}, f32[262144]{0:T(1024)}, /*index=5*/f32[262144]{0:T(1024)}, f32[262144]{0:T(1024)}, f32[262144]{0:T(1024)}) fusion(f32[262144]{0:T(1024)} %bitcast.334, f32[262144]{0:T(1024)S(1)} %bitcast.326, f32[262144]{0:T(1024)} %bitcast.335, ...), kind=kLoop, calls=%fused_computation.81 | loop fusion | flops 4194304 | bytes 26214400 | tf_op jit(solution)/shard_map/vmap()/add | solution.py:158
  (356 shorter events, 125.3 us)
Async XLA Ops:
  7.2 196.0 %all-gather.4.cloned.1.call-start = ((), (), s32[]{:S(2)}) async-start(), calls=%async_computation.1 | async-start | bytes 17825792 | tf_op jit(solution)/shard_map/all_gather | solution.py:21
  9.2 10.6 %collective-permute-start = (bf16[3,1536]{1,0:T(4,128)(2,1)S(1)}, bf16[3,1536]{1,0:T(4,128)(2,1)S(1)}, u32[]{:S(2)}, u32[]{:S(2)}) collective-permute-start(bf16[3,1536]{1,0:T(4,128)(2,1)S(1)} %pad_maximum_fusion.3), channel_id=1, source_target_pairs={{0,8},{8,16},{16,24},{24,32},{32,40},{40,48},{48,56},{56,64},{64,7... | collective-permute-start | bytes 27656 | tf_op jit(solution)/shard_map/ppermute | solution.py:16
  13.6 16.3 %copy-start.17 = (f32[1,1024]{1,0:T(1,128)}, f32[1,1024]{1,0:T(1,128)S(1)}, u32[]{:S(2)}) copy-start(f32[1,1024]{1,0:T(1,128)S(1)} %get-tuple-element.487) | copy-start | bytes 12292
  13.6 16.3 %copy-start.19 = (f32[1,1024]{1,0:T(1,128)}, f32[1,1024]{1,0:T(1,128)S(1)}, u32[]{:S(2)}) copy-start(f32[1,1024]{1,0:T(1,128)S(1)} %get-tuple-element.488) | copy-start | bytes 12292
  13.6 16.3 %copy-start.21 = (f32[1,1024]{1,0:T(1,128)}, f32[1,1024]{1,0:T(1,128)S(1)}, u32[]{:S(2)}) copy-start(f32[1,1024]{1,0:T(1,128)S(1)} %get-tuple-element.489) | copy-start | bytes 12292
  13.6 16.3 %copy-start.23 = (f32[1,1024]{1,0:T(1,128)}, f32[1,1024]{1,0:T(1,128)S(1)}, u32[]{:S(2)}) copy-start(f32[1,1024]{1,0:T(1,128)S(1)} %get-tuple-element.490) | copy-start | bytes 12292
  15.0 14.9 %copy-start.14 = (f32[768]{0:T(1024)}, f32[768]{0:T(1024)S(1)}, u32[]{:S(2)}) copy-start(f32[768]{0:T(1024)S(1)} %get-tuple-element.519) | copy-start | bytes 9220
  15.0 14.9 %copy-start.15 = (f32[768]{0:T(1024)}, f32[768]{0:T(1024)S(1)}, u32[]{:S(2)}) copy-start(f32[768]{0:T(1024)S(1)} %get-tuple-element.520) | copy-start | bytes 9220
  15.0 14.9 %copy-start.16 = (f32[768]{0:T(1024)}, f32[768]{0:T(1024)S(1)}, u32[]{:S(2)}) copy-start(f32[768]{0:T(1024)S(1)} %get-tuple-element.521) | copy-start | bytes 9220
  39.3 39.4 %copy-start.32 = (f32[16]{0:T(128)S(1)}, f32[16]{0:T(128)}, u32[]{:S(2)}) copy-start(f32[16]{0:T(128)} %custom-call) | copy-start | bytes 196
  78.8 5.7 %copy-start.36 = (f32[16]{0:T(128)S(1)}, f32[16]{0:T(128)}, u32[]{:S(2)}) copy-start(f32[16]{0:T(128)} %param.27) | copy-start | bytes 196
  78.8 5.7 %copy-start.38 = (f32[16]{0:T(128)S(1)}, f32[16]{0:T(128)}, u32[]{:S(2)}) copy-start(f32[16]{0:T(128)} %copy-done.37) | copy-start | bytes 196
  84.2 255.7 %all-reduce.4.cloned.1.call-start = ((), (), s32[]{:S(2)}) async-start(), calls=%async_computation | async-start | bytes 2138112 | tf_op jit(solution)/shard_map/psum | solution.py:38
  251.8 89.4 %copy-start.33 = (bf16[1,8,1,512]{3,1,2,0:T(8,128)(2,1)S(1)}, bf16[1,8,1,512]{3,1,2,0:T(8,128)(2,1)}, u32[]{:S(2)}) copy-start(bf16[1,8,1,512]{3,1,2,0:T(8,128)(2,1)} %param.32) | copy-start | bytes 24580
  251.8 89.6 %copy-start.18 = (f32[1,1024]{1,0:T(1,128)S(1)}, f32[1,1024]{1,0:T(1,128)}, u32[]{:S(2)}) copy-start(f32[1,1024]{1,0:T(1,128)} %copy-done.17) | copy-start | bytes 12292
  251.9 89.6 %copy-start.20 = (f32[1,1024]{1,0:T(1,128)S(1)}, f32[1,1024]{1,0:T(1,128)}, u32[]{:S(2)}) copy-start(f32[1,1024]{1,0:T(1,128)} %copy-done.19) | copy-start | bytes 12292
  251.9 89.6 %copy-start.22 = (f32[1,1024]{1,0:T(1,128)S(1)}, f32[1,1024]{1,0:T(1,128)}, u32[]{:S(2)}) copy-start(f32[1,1024]{1,0:T(1,128)} %copy-done.21) | copy-start | bytes 12292
  251.9 89.6 %copy-start.24 = (f32[1,1024]{1,0:T(1,128)S(1)}, f32[1,1024]{1,0:T(1,128)}, u32[]{:S(2)}) copy-start(f32[1,1024]{1,0:T(1,128)} %copy-done.23) | copy-start | bytes 12292
  251.9 89.6 %copy-start.31 = (bf16[1,8,1024]{2,1,0:T(8,128)(2,1)S(1)}, bf16[1,8,1024]{2,1,0:T(8,128)(2,1)}, u32[]{:S(2)}) copy-start(bf16[1,8,1024]{2,1,0:T(8,128)(2,1)} %param.31) | copy-start | bytes 49156
  365.9 5.7 %copy-start.10 = (f32[262144]{0:T(1024)S(1)}, f32[262144]{0:T(1024)}, u32[]{:S(2)}) copy-start(f32[262144]{0:T(1024)} %get-tuple-element.468) | copy-start | bytes 3145732
  368.3 6.5 %copy-start.9 = (f32[262144]{0:T(1024)S(1)}, f32[262144]{0:T(1024)}, u32[]{:S(2)}) copy-start(f32[262144]{0:T(1024)} %get-tuple-element.467) | copy-start | bytes 3145732
  371.6 6.5 %copy-start.8 = (f32[262144]{0:T(1024)S(1)}, f32[262144]{0:T(1024)}, u32[]{:S(2)}) copy-start(f32[262144]{0:T(1024)} %get-tuple-element.466) | copy-start | bytes 3145732
  374.8 6.8 %copy-start.7 = (f32[262144]{0:T(1024)S(1)}, f32[262144]{0:T(1024)}, u32[]{:S(2)}) copy-start(f32[262144]{0:T(1024)} %get-tuple-element.465) | copy-start | bytes 3145732
  378.1 6.8 %copy-start.6 = (f32[262144]{0:T(1024)S(1)}, f32[262144]{0:T(1024)}, u32[]{:S(2)}) copy-start(f32[262144]{0:T(1024)} %get-tuple-element.464) | copy-start | bytes 3145732
  (23 other events, 85.5 us)
Sparse Core Ops, SparseCore 0:
  84.3 118.8 all-gather.3
  243.3 96.6 all-reduce.3
where the time goes:
time: 398 us; the launch traced here: 396 us
  waiting for transfers between devices  151 us (38%)
  local copies, waits for them, and re-layouts  73.4 us (18%)
  other arithmetic  69.5 us (17%)
  matrix products  39.6 us (10%)
  blocking collectives  39 us (10%)
  between operations  15.6 us (4%)
  loops' own time  4.55 us (1%)
    psum x1, waiting for transfers between devices, from_root(): return lax.psum(jnp.where(mine, value, jnp.zeros_like(value)), axis)  86.4 us
    all_gather x1, waiting for transfers between devices, entering(): everything = jax.tree.map(lambda part: lax.all_gather(part, axis), value)  64.4 us
    unnamed x1, blocking collectives  39 us
    unnamed x117, local copies, waits for them, and re-layouts  33.3 us
    select_n x16, other arithmetic, step(): return jax.tree.map(lambda a, b: jnp.where(reached, a, b), new, before)  23.4 us
    dot_general x8, matrix products, decode_one(): jnp.einsum('grpn,gn->grp', current, c_now, precision=lax.Precision.HIGHEST)  12.2 us
    dot_general x3, matrix products, block_terms(): jnp.einsum('kaew,wkal->ekal', mixing_matrix, input_split, preferred_eleme...  10.6 us
    convert_element_type x4, other arithmetic, conv_silu(): return jax.nn.silu(totals).astype(jnp.bfloat16)  9.06 us
  transfers between devices with their start and end apart: 3, of which 2 were waited for; matrix products, arithmetic and copies ran while one was open for 8% of the time, Pallas kernels for 0%

commit v1 on v0

v1 whole, which is shorter than its diff:
```python
import functools

import jax
import jax.numpy as jnp
from jax import lax
from jax.experimental import pallas as pl
from jax.experimental.pallas import tpu as pltpu
from jax.sharding import PartitionSpec as P

BLOCK = 256
TILE = 128
HALO = 16
EPSILON = 1e-05
LOG2E = 1.4426950408889634
MESH = pl.DeviceIdType.MESH
F32 = jnp.float32
BF16 = jnp.bfloat16


def dot(a, b):
    return jnp.dot(a, b, preferred_element_type=F32)


def split3(value):
    high = value.astype(BF16).astype(F32)
    rest = value - high
    middle = rest.astype(BF16).astype(F32)
    low = (rest - middle).astype(BF16).astype(F32)
    return [high, middle, low]


def softplus(value):
    return jnp.maximum(value, 0.0) + jnp.log1p(jnp.exp(-jnp.abs(value)))


def silu(value):
    half = 0.5 * value
    return half + half * jnp.tanh(half)


def conv_chain(rows, taps, linked):
    total = taps[0] * rows
    for tap in taps[1:]:
        total = tap * rows + linked * pltpu.roll(total, 1, 0)
    return total


def kernel(
    seq,
    x_hbm, bc_hbm, dt_hbm, conv_x_hbm, conv_bc_hbm, a_log_hbm, dt_bias_hbm, d_skip_hbm, gain_hbm, doc_hbm,
    dec_x_hbm, dec_bc_hbm, dec_dt_hbm,
    out_hbm, dec_out,
    conv_x, conv_bc, a_log, dt_bias, d_skip, gain, doc, dec_x, dec_bc, dec_dt,
    xbuf, bcbuf, dtbuf, tail_x, tail_bc, xs, xw, bs, cs, bst, expand_a, expand_b, colf, colb, keepb,
    vrow, vecs, part, enter_q, p_msg, p_recv, s_out, s_in, c_msg, c_recv, y_msg, y_recv,
    local, keepx, scm, small, obuf, dec_keep, dec_local,
    few_sem, load_sem, rim_ss, rim_rs, tail_ss, tail_rs, p_ss, p_rs, c_ss, c_rs, s_ss, s_rs, y_ss, y_rs, out_sem,
):
    me = lax.axis_index("seq")
    rows, inner = xs.shape
    blocks = rows // BLOCK
    heads = dtbuf.shape[0]
    width = inner // heads
    pairs = inner // TILE
    state = bs.shape[1]
    docs = doc.shape[0]
    total_rows = rows * seq
    last = seq - 1

    def peer(step):
        return lax.rem(me + step, seq)

    few = [
        (doc_hbm, doc),
        (a_log_hbm, a_log),
        (dt_bias_hbm, dt_bias),
        (d_skip_hbm, d_skip),
        (dt_hbm, dtbuf),
        (conv_x_hbm, conv_x),
        (conv_bc_hbm, conv_bc),
        (gain_hbm, gain),
        (dec_x_hbm, dec_x),
        (dec_bc_hbm, dec_bc),
        (dec_dt_hbm, dec_dt),
    ]
    few = [pltpu.make_async_copy(far, near, few_sem.at[i]) for i, (far, near) in enumerate(few)]
    for copy in few:
        copy.start()
    loads = []
    for b in reversed(range(blocks)):
        there, here = pl.ds(b * BLOCK, BLOCK), pl.ds(HALO + b * BLOCK, BLOCK)
        loads.append(
            (
                pltpu.make_async_copy(x_hbm.at[there], xbuf.at[here], load_sem.at[2 * b]),
                pltpu.make_async_copy(bc_hbm.at[there], bcbuf.at[here], load_sem.at[2 * b + 1]),
            )
        )
        for copy in loads[-1]:
            copy.start()

    barrier = pltpu.get_barrier_semaphore()

    def greet(step, carry):
        pl.semaphore_signal(barrier, inc=1, device_id={"seq": peer(step)}, device_id_type=MESH)
        return carry

    lax.fori_loop(1, seq, greet, 0)

    few[0].wait()
    ends = []
    running = jnp.int32(0)
    for i in range(docs):
        running = running + doc[i]
        ends.append(running)
    base = me * rows

    def start_of(position):
        found = jnp.int32(0)
        for end in ends:
            found = jnp.where(end <= position, jnp.maximum(found, end), found)
        return found

    def next_after(position):
        found = jnp.where(position < 0, jnp.int32(0), jnp.int32(2 * total_rows))
        for end in ends:
            found = jnp.where(end > position, jnp.minimum(found, end), found)
        return found

    def linked_of(positions):
        linked = positions != 0
        for end in ends:
            linked = linked & (positions != end)
        return linked.astype(F32)

    head_row = lax.broadcasted_iota(jnp.int32, (TILE, inner), 0)
    head_of = lax.broadcasted_iota(jnp.int32, (TILE, inner), 1) // width
    expand_a[...] = ((head_row < 3 * heads) & (lax.rem(head_row, heads) == head_of)).astype(BF16)
    expand_b[...] = (
        (head_row >= 3 * heads) & (head_row < 6 * heads) & (lax.rem(head_row, heads) == head_of)
    ).astype(BF16)
    upper = (
        lax.broadcasted_iota(jnp.int32, (BLOCK, BLOCK), 0)
        <= lax.broadcasted_iota(jnp.int32, (BLOCK, BLOCK), 1)
    ).astype(BF16)
    lane = lax.broadcasted_iota(jnp.int32, (heads, TILE), 1)

    for copy in few[1:5]:
        copy.wait()
    small[...] = jnp.zeros_like(small)
    small[0:1, 0:heads] = a_log[...]
    small[1:2, 0:heads] = dt_bias[...]
    small[2:3, 0:heads] = d_skip[...]
    columns = small[...].T
    rate = jnp.exp(columns[0:heads, 0:1]) * LOG2E
    bias = columns[0:heads, 1:2]
    skip = columns[0:heads, 2:3]

    steps = [softplus(dtbuf[:, b * BLOCK : (b + 1) * BLOCK] + bias) for b in range(blocks)]
    parts = []
    for step in steps:
        parts += split3(-step * rate)
    sums = dot(jnp.concatenate(parts, axis=0).astype(BF16), upper)
    before = jnp.zeros((heads, 1), F32)
    whole = jnp.ones((heads, 1), F32)
    throughs = []
    dev_next = next_after(base - 1)
    for b in range(blocks):
        at = 3 * b * heads
        cum = sums[at : at + heads] + sums[at + heads : at + 2 * heads] + sums[at + 2 * heads : at + 3 * heads]
        step = steps[b]
        first = base + b * BLOCK
        end = first + BLOCK - 1
        position = first + lax.broadcasted_iota(jnp.int32, (heads, BLOCK), 1)
        cum_end = cum[:, BLOCK - 1 : BLOCK]
        inflow = jnp.where(position >= start_of(end), jnp.exp2(cum_end - cum) * step, 0.0)
        keep_dev = jnp.where(position < dev_next, jnp.exp2(cum + before), 0.0)
        table = jnp.concatenate(
            split3(inflow) + split3(keep_dev) + [cum, jnp.zeros((TILE - 7 * heads, BLOCK), F32)], axis=0
        ).T
        here = pl.ds(b * BLOCK, BLOCK)
        colf[here] = table
        colb[here] = table.astype(BF16)
        vrow[b] = cum - jnp.log2(step)
        block_next = next_after(first - 1)
        if b:
            keep = jnp.where(position < block_next, jnp.exp2(cum), 0.0)
            keepb[b - 1] = (
                jnp.concatenate(split3(keep) + [jnp.zeros((TILE - 3 * heads, BLOCK), F32)], axis=0)
                .T.astype(BF16)
            )
        throughs.append(jnp.where(end < block_next, jnp.exp2(cum_end), 0.0))
        before = before + cum_end
    whole = jnp.where(base + rows - 1 < dev_next, jnp.exp2(before), 0.0)
    picked = jnp.zeros((heads, TILE), F32)
    for i, column in enumerate([whole, skip] + throughs):
        picked = jnp.where(lane == i, column, picked)
    picked = jnp.concatenate(split3(picked) + [jnp.zeros((TILE - 3 * heads, TILE), F32)], axis=0)
    vecs[...] = dot(picked.T.astype(BF16), expand_a[...])[0:8]

    for copy in few[5:]:
        copy.wait()
    for copy in loads[0]:
        copy.wait()
    pl.semaphore_wait(barrier, seq - 1)
    edge = pl.ds(rows, HALO)

    def rim_copies(to):
        return [
            pltpu.make_async_remote_copy(
                src_ref=buf.at[edge], dst_ref=buf.at[pl.ds(0, HALO)], send_sem=rim_ss.at[i],
                recv_sem=rim_rs.at[i], device_id={"seq": to}, device_id_type=MESH,
            )
            for i, buf in enumerate((xbuf, bcbuf))
        ]

    def tail_copies(to):
        return [
            pltpu.make_async_remote_copy(
                src_ref=buf.at[edge], dst_ref=tail, send_sem=tail_ss.at[i, to],
                recv_sem=tail_rs.at[i], device_id={"seq": to}, device_id_type=MESH,
            )
            for i, (buf, tail) in enumerate(((xbuf, tail_x), (bcbuf, tail_bc)))
        ]

    @pl.when(me < last)
    def _():
        for copy in rim_copies(me + 1):
            copy.start()

    @pl.when(me == last)
    def _():
        def send(to, carry):
            for copy in tail_copies(to):
                copy.start()
            return carry

        lax.fori_loop(0, last, send, 0)
        tail_x[...] = xbuf[edge]
        tail_bc[...] = bcbuf[edge]

    @pl.when(me == 0)
    def _():
        xbuf[pl.ds(0, HALO)] = jnp.zeros((HALO, inner), BF16)
        bcbuf[pl.ds(0, HALO)] = jnp.zeros((HALO, 2 * state), BF16)

    def linked_rows(row):
        positions = base + row - 8 + lax.broadcasted_iota(jnp.int32, (TILE + 8, TILE), 0)
        return linked_of(positions)

    def conv_tile(buf, taps, row, at, linked):
        lanes = slice(at, at + TILE)
        raw = buf[pl.ds(row, TILE + HALO), lanes].astype(F32)[HALO - 8 :]
        return silu(conv_chain(raw, [tap[:, lanes] for tap in taps], linked)[8:]).astype(BF16)

    x_taps = [conv_x[k : k + 1, :] for k in range(4)]
    bc_taps = [conv_bc[k] for k in range(4)]

    def conv_rows(row):
        here = pl.ds(row, TILE)
        linked = linked_rows(row)
        scales = colb[here]
        for p in range(pairs):
            lanes = slice(p * TILE, (p + 1) * TILE)
            value = conv_tile(xbuf, x_taps, row, p * TILE, linked)
            xs[here, lanes] = value
            xw[here, lanes] = (value.astype(F32) * dot(scales, expand_a[:, lanes])).astype(BF16)
        for at in range(0, state, TILE):
            value = conv_tile(bcbuf, bc_taps, row, at, linked)
            bs[here, at : at + TILE] = value
            bst[at : at + TILE, here] = value.astype(F32).T.astype(BF16)

    def conv_c_rows(row):
        here = pl.ds(row, TILE)
        linked = linked_rows(row)
        for at in range(0, state, TILE):
            cs[here, at : at + TILE] = conv_tile(bcbuf, bc_taps, row, state + at, linked)

    def block_part(b):
        here = pl.ds(b * BLOCK, BLOCK)
        for at in range(0, inner, 256):
            part[b, :, at : at + 256] = dot(bst[:, here], xw[here, at : at + 256])

    for b in reversed(range(blocks)):
        if b:
            for copy in loads[blocks - b]:
                copy.wait()
        else:

            @pl.when(me > 0)
            def _():
                for copy in rim_copies(me):
                    copy.wait_recv()

        for row in range(b * BLOCK, (b + 1) * BLOCK, TILE):
            conv_rows(row)
        block_part(b)

    decays = jnp.concatenate(split3(vecs[0:1, :]) + [jnp.zeros((HALO - 3, inner), F32)], axis=0).astype(BF16)
    for p in range(pairs):
        lanes = slice(p * TILE, (p + 1) * TILE)
        value = part[0, :, lanes]
        for b in range(1, blocks):
            enter_q[b - 1, :, lanes] = value.astype(BF16)
            value = vecs[2 + b : 3 + b, lanes] * value + part[b, :, lanes]
        value = value.astype(BF16)
        for half in range(2):
            p_msg[2 * p + half, 0:TILE] = value[half * TILE : (half + 1) * TILE]
            p_msg[2 * p + half, TILE:] = decays[:, lanes]

    def p_copy(step, to):
        return pltpu.make_async_remote_copy(
            src_ref=p_msg.at[to], dst_ref=p_recv.at[me], send_sem=p_ss.at[step],
            recv_sem=p_rs.at[step], device_id={"seq": to}, device_id_type=MESH,
        )

    def c_copy(step, to):
        return pltpu.make_async_remote_copy(
            src_ref=c_msg.at[lax.rem(to, 2)], dst_ref=c_recv.at[me], send_sem=c_ss.at[step],
            recv_sem=c_rs.at[step], device_id={"seq": to}, device_id_type=MESH,
        )

    def s_copy(step, to):
        return pltpu.make_async_remote_copy(
            src_ref=s_out.at[to], dst_ref=s_in.at[me], send_sem=s_ss.at[step],
            recv_sem=s_rs.at[step], device_id={"seq": to}, device_id_type=MESH,
        )

    def y_copy(step, to):
        return pltpu.make_async_remote_copy(
            src_ref=y_msg.at[to], dst_ref=y_recv.at[me], send_sem=y_ss.at[step],
            recv_sem=y_rs.at[step], device_id={"seq": to}, device_id_type=MESH,
        )

    def every(action):
        def body(step, carry):
            action(step, peer(step))
            return carry

        lax.fori_loop(1, seq, body, 0)

    every(lambda step, to: p_copy(step, to).start())
    p_recv[me] = p_msg[me]

    @pl.when(me != last)
    def _():
        for copy in tail_copies(me):
            copy.wait_recv()

    offsets = lax.broadcasted_iota(jnp.int32, (16, TILE), 0)
    tail_doc = jnp.int32(0)
    for end in ends:
        tail_doc = tail_doc + (end <= total_rows - 1).astype(jnp.int32)
    joined = (tail_doc == docs - 1).astype(F32)
    dec_linked = jnp.where(
        offsets < 8, linked_of(total_rows - 8 + offsets), jnp.where(offsets == 8, joined, 1.0)
    )

    def dec_conv(tail, given, taps, at):
        lanes = slice(at, at + TILE)
        ext = jnp.concatenate([tail[:, lanes].astype(F32)[8:], given[:, lanes].astype(F32)], axis=0)
        return silu(conv_chain(ext, [tap[:, lanes] for tap in taps], dec_linked)[8:]).astype(BF16).astype(F32)

    dec_bcs = [dec_conv(tail_bc, dec_bc, bc_taps, at) for at in range(0, 2 * state, TILE)]
    for i in range(2):
        c_msg[i] = jnp.concatenate([dec_bcs[2 + i], jnp.zeros((8, TILE), F32)], axis=0).astype(BF16)
    every(lambda step, to: c_copy(step, to).start())
    c_recv[me] = c_msg[lax.rem(me, 2)]

    def lane_dot(a, b):
        return lax.dot_general(a, b, (((1,), (1,)), ((), ())), preferred_element_type=F32)

    dec_c = jnp.concatenate(dec_bcs[2:], axis=1).astype(BF16)
    dec_b = jnp.concatenate(dec_bcs[:2], axis=1).astype(BF16)
    dec_scores = lane_dot(dec_c, dec_b)
    dec_step = softplus(dec_dt[...] + dt_bias[...])
    dec_cum = -dec_step * jnp.exp(a_log[...])
    dec_row = lax.broadcasted_iota(jnp.int32, (8, heads), 0)
    for shift in (1, 2, 4):
        dec_cum = dec_cum + jnp.where(dec_row >= shift, pltpu.roll(dec_cum, shift, 0), 0.0)
    factors = []
    for s in range(8):
        gap = jnp.where(dec_row >= s, dec_cum - dec_cum[s : s + 1], 0.0)
        weight = dec_scores[:, s : s + 1] * jnp.exp(gap) * dec_step[s : s + 1]
        factors.append(jnp.where(dec_row >= s, weight, 0.0))
    factors.append(jnp.exp(dec_cum))
    factors = jnp.concatenate(factors, axis=0)
    factors = jnp.concatenate(
        split3(factors) + [jnp.zeros((factors.shape[0], TILE - 3 * heads), F32)], axis=1
    ).astype(BF16)
    for p in range(pairs):
        lanes = slice(p * TILE, (p + 1) * TILE)
        wide = dot(factors, expand_a[:, lanes])
        given = dec_conv(tail_x, dec_x, x_taps, p * TILE)
        answer = vecs[1:2, lanes] * given
        for s in range(8):
            answer = answer + wide[8 * s : 8 * s + 8] * given[s : s + 1]
        dec_local[:, lanes] = answer
        dec_keep[:, lanes] = wide[64:72]

    left_half = lax.broadcasted_iota(jnp.int32, (BLOCK, TILE), 1) < width

    def block_scores(b):
        here = pl.ds(b * BLOCK, BLOCK)
        row = lax.broadcasted_iota(jnp.int32, (BLOCK, BLOCK), 0)
        col = lax.broadcasted_iota(jnp.int32, (BLOCK, BLOCK), 1)
        first = base + b * BLOCK
        starts = jnp.zeros((BLOCK, BLOCK), jnp.int32)
        for end in ends:
            starts = jnp.where(row >= end - first, jnp.maximum(starts, end - first), starts)
        scm[...] = jnp.where((col <= row) & (col >= starts), dot(cs[here], bst[:, here]), 0.0)

    def block_local(b):
        here = pl.ds(b * BLOCK, BLOCK)
        block_scores(b)
        top, low = slice(0, TILE), slice(TILE, BLOCK)
        for p in range(pairs):
            lanes = slice(p * TILE, (p + 1) * TILE)
            value = xs[here, lanes]
            zero = jnp.zeros_like(value)
            sides = [jnp.where(left_half, value, zero), jnp.where(left_half, zero, value)]
            tops, lows = [], []
            for head in (2 * p, 2 * p + 1):
                cum_col = colf[here, 6 * heads + head : 6 * heads + head + 1]
                v = vrow[b, head : head + 1, :]
                gap = jnp.minimum(cum_col[top] - v[:, :TILE], 126.0)
                tops.append((scm[top, :TILE] * jnp.exp2(gap)).astype(BF16))
                gap = jnp.minimum(cum_col[low] - v, 126.0)
                lows.append((scm[low, :] * jnp.exp2(gap)).astype(BF16))
            inner_top = dot(
                jnp.concatenate(tops, axis=1), jnp.concatenate([side[top] for side in sides], axis=0)
            )
            inner_low = dot(jnp.concatenate(lows, axis=1), jnp.concatenate(sides, axis=0))
            answer = jnp.concatenate([inner_top, inner_low], axis=0) + vecs[1:2, lanes] * value.astype(F32)
            if b:
                carried = dot(cs[here], enter_q[b - 1, :, lanes])
                answer = answer + dot(keepb[b - 1], expand_a[:, lanes]) * carried
            local[here, lanes] = answer
            keepx[here, lanes] = dot(colb[here], expand_b[:, lanes])

    for row in range(0, rows, TILE):
        conv_c_rows(row)
    for b in range(blocks - 1):
        block_local(b)

    def scan(k, value):
        step = lax.rem(me - k + seq, seq)

        @pl.when(k != me)
        def _():
            p_copy(step, me).wait_recv()

        s_out[k] = value.astype(BF16)
        tags = p_recv[k, TILE:].astype(F32)
        decay = tags[0:1] + tags[1:2] + tags[2:3]
        return decay * value + p_recv[k, 0:TILE].astype(F32)

    final = lax.fori_loop(0, seq, scan, jnp.zeros((TILE, TILE), F32))
    every(lambda step, to: s_copy(step, to).start())
    s_in[me] = s_out[me]
    every(lambda step, to: c_copy(step, to).wait_recv())
    asked = c_recv[...].reshape(seq * 16, TILE)
    replies = sum(dot(asked, piece.astype(BF16)) for piece in split3(final))
    y_msg[...] = replies.reshape(seq, 16, TILE)[:, 0:8]
    every(lambda step, to: y_copy(step, to).start())
    y_recv[me] = y_msg[me]

    block_local(blocks - 1)

    def norm(pieces):
        squares = sum(piece * piece for piece in pieces)
        scale = lax.rsqrt(jnp.sum(squares, axis=1, keepdims=True) / inner + EPSILON)
        return [piece * scale for piece in pieces]

    every(lambda step, to: y_copy(step, to).wait_recv())
    pieces = []
    for p in range(pairs):
        lanes = slice(p * TILE, (p + 1) * TILE)
        pieces.append(dec_local[:, lanes] + dec_keep[:, lanes] * (y_recv[2 * p] + y_recv[2 * p + 1]))
    for p, piece in enumerate(norm(pieces)):
        lanes = slice(p * TILE, (p + 1) * TILE)
        dec_out[:, lanes] = (piece * gain[:, lanes]).astype(BF16)

    every(lambda step, to: s_copy(step, to).wait_recv())

    def finish(i, carry):
        row = pl.multiple_of(i * TILE, TILE)
        here = pl.ds(row, TILE)
        readout = cs[here]
        pieces = []
        for q in range(pairs // 2):
            entering = jnp.concatenate(
                [
                    jnp.concatenate([s_in[4 * q], s_in[4 * q + 1]], axis=0),
                    jnp.concatenate([s_in[4 * q + 2], s_in[4 * q + 3]], axis=0),
                ],
                axis=1,
            )
            lanes = slice(q * 256, (q + 1) * 256)
            pieces.append(local[here, lanes] + keepx[here, lanes] * dot(readout, entering))
        squares = sum(jnp.sum(piece * piece, axis=1, keepdims=True) for piece in pieces)
        scale = lax.rsqrt(squares / inner + EPSILON)
        for q, piece in enumerate(pieces):
            lanes = slice(q * 256, (q + 1) * 256)
            obuf[here, lanes] = (piece * scale * gain[:, lanes]).astype(BF16)
        pltpu.make_async_copy(obuf.at[here], out_hbm.at[here], out_sem.at[i]).start()
        return carry

    lax.fori_loop(0, rows // TILE, finish, 0)

    @pl.when(me < last)
    def _():
        for copy in rim_copies(me + 1):
            copy.wait_send()

    @pl.when(me == last)
    def _():
        def sent(to, carry):
            for copy in tail_copies(to):
                copy.wait_send()
            return carry

        lax.fori_loop(0, last, sent, 0)

    def settle(step, to):
        for copy in (p_copy, c_copy, s_copy, y_copy):
            copy(step, to).wait_send()

    every(settle)

    def written(i, carry):
        here = pl.ds(pl.multiple_of(i * TILE, TILE), TILE)
        pltpu.make_async_copy(obuf.at[here], out_hbm.at[here], out_sem.at[i]).wait()
        return carry

    lax.fori_loop(0, rows // TILE, written, 0)


def body(
    x_in, bc_in, dt_in, conv_x, conv_bc, a_log, dt_bias, d_skip, norm_gain, doc_lengths, dec_x, dec_bc, dec_dt
):
    rows, inner = x_in.shape
    heads = dt_in.shape[1]
    double = bc_in.shape[2]
    state = double // 2
    seq = lax.axis_size("seq")
    blocks = rows // BLOCK
    whole = pl.BlockSpec(memory_space=pl.ANY)
    near = pl.BlockSpec(memory_space=pltpu.VMEM)
    dma = pltpu.SemaphoreType.DMA
    vmem = pltpu.VMEM
    prompt, decoded = pl.pallas_call(
        functools.partial(kernel, seq),
        out_shape=(
            jax.ShapeDtypeStruct((rows, inner), BF16),
            jax.ShapeDtypeStruct((8, inner), BF16),
        ),
        in_specs=[whole] * 13,
        out_specs=(whole, near),
        scratch_shapes=[
            vmem(conv_x.shape, F32),
            vmem(conv_bc.shape, F32),
            vmem((1, heads), F32),
            vmem((1, heads), F32),
            vmem((1, heads), F32),
            vmem((1, inner), F32),
            pltpu.SMEM(doc_lengths.shape, jnp.int32),
            vmem((8, inner), BF16),
            vmem((8, double), BF16),
            vmem((8, heads), F32),
            vmem((HALO + rows, inner), BF16),
            vmem((HALO + rows, double), BF16),
            vmem((heads, rows), F32),
            vmem((HALO, inner), BF16),
            vmem((HALO, double), BF16),
            vmem((rows, inner), BF16),
            vmem((rows, inner), BF16),
            vmem((rows, state), BF16),
            vmem((rows, state), BF16),
            vmem((state, rows), BF16),
            vmem((TILE, inner), BF16),
            vmem((TILE, inner), BF16),
            vmem((rows, TILE), F32),
            vmem((rows, TILE), BF16),
            vmem((blocks - 1, BLOCK, TILE), BF16),
            vmem((blocks, heads, BLOCK), F32),
            vmem((8, inner), F32),
            vmem((blocks, state, inner), F32),
            vmem((blocks - 1, state, inner), BF16),
            vmem((seq, TILE + HALO, TILE), BF16),
            vmem((seq, TILE + HALO, TILE), BF16),
            vmem((seq, TILE, TILE), BF16),
            vmem((seq, TILE, TILE), BF16),
            vmem((2, 16, TILE), BF16),
            vmem((seq, 16, TILE), BF16),
            vmem((seq, 8, TILE), F32),
            vmem((seq, 8, TILE), F32),
            vmem((rows, inner), F32),
            vmem((rows, inner), F32),
            vmem((BLOCK, BLOCK), F32),
            vmem((TILE, TILE), F32),
            vmem((rows, inner), BF16),
            vmem((8, inner), F32),
            vmem((8, inner), F32),
            dma((11,)),
            dma((2 * blocks,)),
            dma((2,)),
            dma((2,)),
            dma((2, seq)),
            dma((2,)),
        ]
        + [dma((seq,))] * 8
        + [dma((rows // TILE,))],
        compiler_params=pltpu.CompilerParams(
            collective_id=0, has_side_effects=True, vmem_limit_bytes=60 << 20
        ),
    )(
        x_in,
        bc_in.reshape(rows, double),
        dt_in.T,
        conv_x,
        conv_bc,
        a_log.reshape(1, heads),
        dt_bias.reshape(1, heads),
        d_skip.reshape(1, heads),
        norm_gain.reshape(1, inner),
        doc_lengths,
        dec_x.reshape(8, inner),
        dec_bc.reshape(8, double),
        dec_dt.reshape(8, heads),
    )
    return prompt, decoded.reshape(1, 8, inner)


def solution(mesh):
    placed = (
        P(("group", "seq"), "head"),
        P(("group", "seq"), "head", None),
        P(("group", "seq"), "head"),
        P(None, "head"),
        P(None, "head", None),
        P("head"),
        P("head"),
        P("head"),
        P("head"),
        P("group"),
        P(("group", "seq"), None, "head"),
        P(("group", "seq"), None, "head", None),
        P(("group", "seq"), None, "head"),
    )
    return jax.shard_map(
        body,
        mesh=mesh,
        in_specs=placed,
        out_specs=(P(("group", "seq"), "head"), P(("group", "seq"), None, "head")),
        check_vma=False,
    )
```

time: 398 us -> 39.5 us (0.10)
  waiting for transfers between devices: 151 us -> 0 us
  local copies, waits for them, and re-layouts: 73.4 us -> 3.28 us
  other arithmetic: 69.5 us -> 0 us
  matrix products: 39.6 us -> 0 us
  blocking collectives: 39 us -> 0 us
  Pallas kernels: 0 us -> 35.5 us
  between operations: 15.6 us -> 0.65 us
  loops' own time: 4.55 us -> 0 us
    psum x1 -> x0, waiting for transfers between devices: 86.4 us -> none  [from_root(): return lax.psum(jnp.where(mine, value, jnp.zeros_like(value)), axis)]
    all_gather x1 -> x0, waiting for transfers between devices: 64.4 us -> none  [entering(): everything = jax.tree.map(lambda part: lax.all_gather(part, axis), value)]
    dot_general x20 -> x0, matrix products: 39.6 us -> none  [the longest x8 12.2 us: decode_one(): jnp.einsum('grpn,gn->grp', current, c_now, precision=lax.Precision.HIGHEST)]
    unnamed x1 -> x0, blocking collectives: 39 us -> none
    pallas_call x0 -> x1, Pallas kernels: none -> 35.5 us  [body(): pl.pallas_call(functools.partial(kernel, seq), out_shape=(jax.ShapeDtypeS...]
    unnamed x117 -> x4, local copies, waits for them, and re-layouts: 33.3 us -> 3.28 us
    select_n x20 -> x0, other arithmetic: 24.4 us -> none  [the longest x16 23.4 us: step(): return jax.tree.map(lambda a, b: jnp.where(reached, a, b), new, before)]
    add x10 -> x0, other arithmetic: 17.7 us -> none  [the longest x1 8.92 us: decode_one(): decay_now[:, :, None, None] * current]
  transfers between devices with their start and end apart: 3 -> 0, of which waited for: 2 -> 0; matrix products, arithmetic and copies ran while one was open for 8% -> 0% of each run, Pallas kernels for 0% -> 0%
where the time goes in v1:
time: 39.5 us; the launch traced here: 39.4 us
  Pallas kernels  35.5 us (90%)
  local copies, waits for them, and re-layouts  3.28 us (8%)
  between operations  0.65 us (2%)
    pallas_call x1, Pallas kernels, body(): pl.pallas_call(functools.partial(kernel, seq), out_shape=(jax.ShapeDtypeS...  35.5 us
    unnamed x4, local copies, waits for them, and re-layouts  3.28 us

profile of v1, /device:TPU:32, one launch (start us, length us, event | category | flops | bytes accessed | tf_op | source)
XLA Modules:
  0.0 39.4 jit_solution(4314444222385167683)
XLA Ops:
  0.6 35.5 %shard_map.140 = (bf16[768,1024]{1,0:T(8,128)(2,1)}, bf16[8,1024]{1,0:T(8,128)(2,1)}) custom-call(bf16[768,1024]{1,0:T(8,128)(2,1)} %x_hbm.1, bf16[768,512]{1,0:T(8,128)(2,1)} %bitcast.10, f32[16,768]{1,0:T(8,128)} %bitcast.11, f32[4,1024]{1,0:T(4,128)} %conv_x_hbm.1, f32[4,1,512]{2,1,0:T(1,128)} %conv_bc_hbm.1, f32[1,16]{1,0:T(1,128)} %bitcast.17, ...), custom_call_target="tpu_custom_call" | custom-call | tf_op jit(solution)/shard_map/pallas_call | solution.py:551
  36.1 0.0 copy-start
  36.1 2.7 %copy.17 = bf16[768,1024]{1,0:T(8,128)(2,1)} copy(bf16[768,1024]{1,0:T(8,128)(2,1)} %get-tuple-element.8) | data formatting | bytes 3145728
  38.8 0.0 copy-done
  38.8 0.6 %copy.18 = bf16[1,8,1024]{2,1,0:T(8,128)(2,1)} copy(bf16[1,8,1024]{2,1,0:T(8,128)(2,1)S(1)} %bitcast.13) | data formatting | bytes 32768
Async XLA Ops:
  36.1 2.7 %copy-start = (bf16[8,1024]{1,0:T(8,128)(2,1)S(1)}, bf16[8,1024]{1,0:T(8,128)(2,1)}, u32[]{:S(2)}) copy-start(bf16[8,1024]{1,0:T(8,128)(2,1)} %get-tuple-element.5) | copy-start | bytes 49156

commit v2 on v1

v2 whole, which is shorter than its diff:
```python
import functools

import jax
import jax.numpy as jnp
from jax import lax
from jax.experimental import pallas as pl
from jax.experimental.pallas import tpu as pltpu
from jax.sharding import PartitionSpec as P

BLOCK = 256
TILE = 128
HALO = 16
EPSILON = 1e-05
LOG2E = 1.4426950408889634
MESH = pl.DeviceIdType.MESH
F32 = jnp.float32
BF16 = jnp.bfloat16


def dot(a, b):
    return jnp.dot(a, b, preferred_element_type=F32)


def split3(value):
    high = value.astype(BF16).astype(F32)
    rest = value - high
    middle = rest.astype(BF16).astype(F32)
    low = (rest - middle).astype(BF16).astype(F32)
    return [high, middle, low]


def softplus(value):
    return jnp.maximum(value, 0.0) + jnp.log1p(jnp.exp(-jnp.abs(value)))


def silu(value):
    half = 0.5 * value
    return half + half * jnp.tanh(half)


def conv_chain(rows, taps, linked):
    total = taps[0] * rows
    for tap in taps[1:]:
        total = tap * rows + linked * pltpu.roll(total, 1, 0)
    return total


def kernel(
    seq,
    x_hbm, bc_hbm, dt_hbm, conv_x_hbm, conv_bc_hbm, a_log_hbm, dt_bias_hbm, d_skip_hbm, gain_hbm, doc_hbm,
    dec_x_hbm, dec_bc_hbm, dec_dt_hbm,
    out, dec_out,
    conv_x, conv_bc, a_log, dt_bias, d_skip, gain, doc, dec_x, dec_bc, dec_dt,
    xbuf, bcbuf, dtbuf, rim_msg, rim_recv, tail_recv, tail_f32, xs, xw, bs, cs, bst, expand_a, expand_b, colf, colb, keepb,
    vrow, vecs, enter_q, p_msg, p_recv, s_out, s_in,
    local, keepx, scm, small, edges, dec_factors, obuf, dec_keep, dec_local,
    few_sem, load_sem, rim_ss, rim_rs, tail_ss, tail_rs, p_ss, p_rs, s_ss, s_rs, out_sem,
):
    me = lax.axis_index("seq")
    rows, inner = xs.shape
    blocks = rows // BLOCK
    heads = dtbuf.shape[0]
    width = inner // heads
    pairs = inner // TILE
    state = bs.shape[1]
    docs = doc.shape[0]
    total_rows = rows * seq
    last = seq - 1

    def peer(step):
        return lax.rem(me + step, seq)

    few = [
        (doc_hbm, doc),
        (a_log_hbm, a_log),
        (dt_bias_hbm, dt_bias),
        (d_skip_hbm, d_skip),
        (dt_hbm, dtbuf),
        (conv_x_hbm, conv_x),
        (conv_bc_hbm, conv_bc),
        (gain_hbm, gain),
        (dec_x_hbm, dec_x),
        (dec_bc_hbm, dec_bc),
        (dec_dt_hbm, dec_dt),
    ]
    few = [pltpu.make_async_copy(far, near, few_sem.at[i]) for i, (far, near) in enumerate(few)]
    for copy in few:
        copy.start()
    loads = []
    for b in reversed(range(blocks)):
        there, here = pl.ds(b * BLOCK, BLOCK), pl.ds(HALO + b * BLOCK, BLOCK)
        loads.append(
            (
                pltpu.make_async_copy(x_hbm.at[there], xbuf.at[here], load_sem.at[2 * b]),
                pltpu.make_async_copy(bc_hbm.at[there], bcbuf.at[here], load_sem.at[2 * b + 1]),
            )
        )
        for copy in loads[-1]:
            copy.start()

    barrier = pltpu.get_barrier_semaphore()

    def greet(step, carry):
        pl.semaphore_signal(barrier, inc=1, device_id={"seq": peer(step)}, device_id_type=MESH)
        return carry

    lax.fori_loop(1, seq, greet, 0)

    few[0].wait()
    ends = []
    running = jnp.int32(0)
    for i in range(docs):
        running = running + doc[i]
        ends.append(running)
    base = me * rows

    def start_of(position):
        found = jnp.int32(0)
        for end in ends:
            found = jnp.where(end <= position, jnp.maximum(found, end), found)
        return found

    def next_after(position):
        found = jnp.where(position < 0, jnp.int32(0), jnp.int32(2 * total_rows))
        for end in ends:
            found = jnp.where(end > position, jnp.minimum(found, end), found)
        return found

    def linked_of(positions):
        linked = positions != 0
        for end in ends:
            linked = linked & (positions != end)
        return linked.astype(F32)

    head_row = lax.broadcasted_iota(jnp.int32, (TILE, inner), 0)
    channel = lax.broadcasted_iota(jnp.int32, (TILE, inner), 1)

    def spread(first):
        found = jnp.zeros((TILE, inner), jnp.bool_)
        for copy_at in range(first, first + 3 * heads, heads):
            low = (head_row - copy_at) * width
            found = found | ((channel >= low) & (channel < low + width) & (head_row >= copy_at))
        return found.astype(BF16)

    expand_a[...] = spread(0)
    expand_b[...] = spread(3 * heads)
    upper = (
        lax.broadcasted_iota(jnp.int32, (BLOCK, BLOCK), 0)
        <= lax.broadcasted_iota(jnp.int32, (BLOCK, BLOCK), 1)
    ).astype(BF16)
    lane = lax.broadcasted_iota(jnp.int32, (heads, TILE), 1)

    for copy in few[1:5]:
        copy.wait()
    small[...] = jnp.zeros_like(small)
    small[0:1, 0:heads] = a_log[...]
    small[1:2, 0:heads] = dt_bias[...]
    small[2:3, 0:heads] = d_skip[...]
    columns = small[...].T
    rate = jnp.exp(columns[0:heads, 0:1]) * LOG2E
    bias = columns[0:heads, 1:2]
    skip = columns[0:heads, 2:3]

    steps = [softplus(dtbuf[:, b * BLOCK : (b + 1) * BLOCK] + bias) for b in range(blocks)]
    parts = []
    for step in steps:
        parts += split3(-step * rate)
    sums = dot(jnp.concatenate(parts, axis=0).astype(BF16), upper)
    before = jnp.zeros((heads, 1), F32)
    whole = jnp.ones((heads, 1), F32)
    throughs = []
    dev_next = next_after(base - 1)
    for b in range(blocks):
        at = 3 * b * heads
        cum = sums[at : at + heads] + sums[at + heads : at + 2 * heads] + sums[at + 2 * heads : at + 3 * heads]
        step = steps[b]
        first = base + b * BLOCK
        end = first + BLOCK - 1
        position = first + lax.broadcasted_iota(jnp.int32, (heads, BLOCK), 1)
        cum_end = cum[:, BLOCK - 1 : BLOCK]
        inflow = jnp.where(position >= start_of(end), jnp.exp2(cum_end - cum) * step, 0.0)
        keep_dev = jnp.where(position < dev_next, jnp.exp2(cum + before), 0.0)
        table = jnp.concatenate(
            split3(inflow) + split3(keep_dev) + [cum, jnp.zeros((TILE - 7 * heads, BLOCK), F32)], axis=0
        ).T
        here = pl.ds(b * BLOCK, BLOCK)
        colf[here] = table
        colb[here] = table.astype(BF16)
        vrow[b] = cum - jnp.log2(step)
        block_next = next_after(first - 1)
        keep = jnp.where(position < block_next, jnp.exp2(cum), 0.0)
        keepb[b] = (
            jnp.concatenate(split3(keep) + [jnp.zeros((TILE - 3 * heads, BLOCK), F32)], axis=0)
            .T.astype(BF16)
        )
        throughs.append(jnp.where(end < block_next, jnp.exp2(cum_end), 0.0))
        before = before + cum_end
    whole = jnp.where(base + rows - 1 < dev_next, jnp.exp2(before), 0.0)
    picked = jnp.zeros((heads, TILE), F32)
    for i, column in enumerate([whole, skip] + throughs):
        picked = jnp.where(lane == i, column, picked)
    picked = jnp.concatenate(split3(picked) + [jnp.zeros((TILE - 3 * heads, TILE), F32)], axis=0)
    vecs[...] = dot(picked.T.astype(BF16), expand_a[...])[0:8]

    for copy in few[5:]:
        copy.wait()
    for copy in loads[0]:
        copy.wait()
    pl.semaphore_wait(barrier, seq - 1)
    edge = pl.ds(rows, HALO)
    pieces = []
    for buf, count in ((xbuf, inner // TILE), (bcbuf, 2 * state // TILE)):
        for t in range(count):
            pieces.append(buf[edge, t * TILE : (t + 1) * TILE].astype(F32)[HALO - 4 :])
    rim_msg[...] = jnp.concatenate(pieces, axis=0).astype(BF16)

    def rim_copy(to):
        return pltpu.make_async_remote_copy(
            src_ref=rim_msg, dst_ref=rim_recv, send_sem=rim_ss.at[0],
            recv_sem=rim_rs.at[0], device_id={"seq": to}, device_id_type=MESH,
        )

    def tail_copy(to):
        return pltpu.make_async_remote_copy(
            src_ref=rim_msg, dst_ref=tail_recv, send_sem=tail_ss.at[to],
            recv_sem=tail_rs.at[0], device_id={"seq": to}, device_id_type=MESH,
        )

    @pl.when(me < last)
    def _():
        rim_copy(me + 1).start()

    @pl.when(me == last)
    def _():
        def send(step, carry):
            tail_copy(last - step).start()
            return carry

        lax.fori_loop(1, seq, send, 0)
        tail_recv[...] = rim_msg[...]

    @pl.when(me == 0)
    def _():
        rim_recv[...] = jnp.zeros_like(rim_recv)

    def linked_rows(row):
        positions = base + row - 8 + lax.broadcasted_iota(jnp.int32, (TILE + 8, TILE), 0)
        return linked_of(positions)

    def conv_tile(buf, taps, row, at, linked):
        lanes = slice(at, at + TILE)
        raw = buf[pl.ds(row, TILE + HALO), lanes].astype(F32)[HALO - 8 :]
        return silu(conv_chain(raw, [tap(lanes) for tap in taps], linked)[8:]).astype(BF16)

    x_taps = [lambda lanes, k=k: conv_x[k : k + 1, lanes] for k in range(4)]
    bc_taps = [lambda lanes, k=k: conv_bc[k, :, lanes] for k in range(4)]

    def conv_rows(i, carry):
        row = pl.multiple_of((rows // TILE - 1 - i) * TILE, TILE)

        @pl.when((row == 0) & (me > 0))
        def _():
            rim_copy(me).wait_recv()

        @pl.when(row == 0)
        def _():
            rim = rim_recv[...].astype(F32)
            blank = jnp.zeros((HALO - 4, TILE), F32)
            at = 0
            for buf, count in ((xbuf, inner // TILE), (bcbuf, 2 * state // TILE)):
                for t in range(count):
                    piece = jnp.concatenate([blank, rim[at : at + 4]], axis=0)
                    buf[0:HALO, t * TILE : (t + 1) * TILE] = piece.astype(BF16)
                    at += 4

        here = pl.ds(row, TILE)
        linked = linked_rows(row)
        for at in range(0, state, TILE):
            value = conv_tile(bcbuf, bc_taps, row, at, linked)
            bs[here, at : at + TILE] = value
            bst[at : at + TILE, here] = value.astype(F32).T.astype(BF16)
        scales = colb[here]
        for p in range(pairs):
            lanes = slice(p * TILE, (p + 1) * TILE)
            value = conv_tile(xbuf, x_taps, row, p * TILE, linked)
            xs[here, lanes] = value
            xw[here, lanes] = (value.astype(F32) * dot(scales, expand_a[:, lanes])).astype(BF16)

        return carry

    def conv_c_rows(i, carry):
        row = pl.multiple_of(i * TILE, TILE)
        linked = linked_rows(row)
        for at in range(0, state, TILE):
            cs[pl.ds(row, TILE), at : at + TILE] = conv_tile(bcbuf, bc_taps, row, state + at, linked)
        return carry

    for pair in loads[1:]:
        for copy in pair:
            copy.wait()
    lax.fori_loop(0, rows // TILE, conv_rows, 0, unroll=2)

    offsets = lax.broadcasted_iota(jnp.int32, (16, TILE), 0)
    tail_doc = jnp.int32(0)
    for end in ends:
        tail_doc = tail_doc + (end <= total_rows - 1).astype(jnp.int32)
    joined = (tail_doc == docs - 1).astype(F32)
    dec_linked = jnp.where(
        offsets < 8, linked_of(total_rows - 8 + offsets), jnp.where(offsets == 8, joined, 1.0)
    )

    def dec_conv(tail_at, given, taps, at):
        lanes = pl.ds(at, TILE)
        ext = jnp.concatenate([tail_f32[pl.ds(tail_at, 8)], given[:, lanes].astype(F32)], axis=0)
        return silu(conv_chain(ext, [tap(lanes) for tap in taps], dec_linked)[8:]).astype(BF16).astype(F32)

    @pl.when(me != last)
    def _():
        tail_copy(me).wait_recv()

    tail = tail_recv[...].astype(F32)
    spaced = []
    for t in range(tail.shape[0] // 4):
        spaced += [jnp.zeros((4, TILE), F32), tail[4 * t : 4 * t + 4]]
    tail_f32[...] = jnp.concatenate(spaced, axis=0)
    dec_bcs = [dec_conv(8 * (pairs + at // TILE), dec_bc, bc_taps, at) for at in range(0, 2 * state, TILE)]

    def p_copy(part, step, to):
        return pltpu.make_async_remote_copy(
            src_ref=p_msg.at[part, to], dst_ref=p_recv.at[part, me], send_sem=p_ss.at[part, step],
            recv_sem=p_rs.at[part, step], device_id={"seq": to}, device_id_type=MESH,
        )

    def s_copy(part, step, to):
        return pltpu.make_async_remote_copy(
            src_ref=s_out.at[part, to], dst_ref=s_in.at[part, me], send_sem=s_ss.at[part, step],
            recv_sem=s_rs.at[part, step], device_id={"seq": to}, device_id_type=MESH,
        )

    def every(action):
        def body(step, carry):
            action(step, peer(step))
            return carry

        lax.fori_loop(1, seq, body, 0)

    edges[...] = jnp.concatenate(split3(vecs[0:1, :]) + [jnp.zeros((5, inner), F32)], axis=0)
    enter_q[0] = jnp.zeros((state, inner), BF16)
    share = state // 4

    def contribute(part):
        for g in range(part * pairs // 4, (part + 1) * pairs // 4):
            lanes = slice(g * BLOCK, (g + 1) * BLOCK)
            value = dot(bst[:, 0:BLOCK], xw[0:BLOCK, lanes])
            for b in range(1, blocks):
                here = slice(b * BLOCK, (b + 1) * BLOCK)
                enter_q[b, :, lanes] = value.astype(BF16)
                value = vecs[2 + b : 3 + b, lanes] * value + dot(bst[:, here], xw[here, lanes])
            value = value.astype(BF16)
            for p in range(2):
                decay = edges[:, g * BLOCK + p * TILE : g * BLOCK + (p + 1) * TILE]
                for quarter in range(4):
                    to = (8 * g + 4 * p + quarter) % seq
                    p_msg[part, to, 0:share] = value[quarter * share : (quarter + 1) * share, p * TILE : (p + 1) * TILE]
                    p_msg[part, to, share:] = jnp.concatenate([decay, dec_bcs[2 + quarter // 2]], axis=0).astype(BF16)

                    @pl.when(to != me)
                    def _(to=to):
                        p_copy(part, lax.rem(to - me + seq, seq), to).start()

        p_recv[part, me] = p_msg[part, me]

    contribute(0)
    contribute(1)
    lax.fori_loop(0, rows // TILE, conv_c_rows, 0, unroll=2)

    def lane_dot(a, b):
        return lax.dot_general(a, b, (((1,), (1,)), ((), ())), preferred_element_type=F32)

    dec_c = jnp.concatenate(dec_bcs[2:], axis=1).astype(BF16)
    dec_b = jnp.concatenate(dec_bcs[:2], axis=1).astype(BF16)
    dec_scores = lane_dot(dec_c, dec_b)
    dec_step = softplus(dec_dt[...] + dt_bias[...])
    dec_cum = -dec_step * jnp.exp(a_log[...])
    dec_row = lax.broadcasted_iota(jnp.int32, (8, heads), 0)
    for shift in (1, 2, 4):
        dec_cum = dec_cum + jnp.where(dec_row >= shift, pltpu.roll(dec_cum, shift, 0), 0.0)
    factors = []
    for s in range(8):
        gap = jnp.where(dec_row >= s, dec_cum - dec_cum[s : s + 1], 0.0)
        weight = dec_scores[:, s : s + 1] * jnp.exp(gap) * dec_step[s : s + 1]
        factors.append(jnp.where(dec_row >= s, weight, 0.0))
    factors.append(jnp.exp(dec_cum))
    factors = jnp.concatenate(factors, axis=0)
    factors = jnp.concatenate(
        split3(factors) + [jnp.zeros((factors.shape[0], TILE - 3 * heads), F32)], axis=1
    ).astype(BF16)
    dec_factors[...] = factors

    def given_pair(p, carry):
        at = pl.multiple_of(p * TILE, TILE)
        lanes = pl.ds(at, TILE)
        wide = dot(dec_factors[...], expand_a[:, lanes])
        given = dec_conv(pl.multiple_of(8 * p, 8), dec_x, x_taps, at)
        answer = vecs[1:2, lanes] * given
        for s in range(8):
            answer = answer + wide[8 * s : 8 * s + 8] * given[s : s + 1]
        dec_local[:, lanes] = answer
        dec_keep[:, lanes] = wide[64:72]
        return carry

    def given_tokens():
        lax.fori_loop(0, pairs, given_pair, 0)


    left_half = lax.broadcasted_iota(jnp.int32, (BLOCK, TILE), 1) < width

    def block_local(b, carry):
        here = pl.ds(pl.multiple_of(b * BLOCK, BLOCK), BLOCK)
        row = lax.broadcasted_iota(jnp.int32, (BLOCK, BLOCK), 0)
        col = lax.broadcasted_iota(jnp.int32, (BLOCK, BLOCK), 1)
        first = base + b * BLOCK
        starts = jnp.zeros((BLOCK, BLOCK), jnp.int32)
        for end in ends:
            starts = jnp.where(row >= end - first, jnp.maximum(starts, end - first), starts)
        scm[...] = jnp.where((col <= row) & (col >= starts), dot(cs[here], bst[:, here]), 0.0)
        top, low = slice(0, TILE), slice(TILE, BLOCK)

        for p in range(pairs):
            lanes = slice(p * TILE, (p + 1) * TILE)
            value = xs[here, lanes]
            zero = jnp.zeros_like(value)
            sides = [jnp.where(left_half, value, zero), jnp.where(left_half, zero, value)]
            tops, lows = [], []
            for side in range(2):
                head = 2 * p + side
                cum_col = colf[here, 6 * heads + head : 6 * heads + head + 1]
                v = vrow[b, head : head + 1, :]
                gap = jnp.minimum(cum_col[top] - v[:, :TILE], 126.0)
                tops.append((scm[top, :TILE] * jnp.exp2(gap)).astype(BF16))
                gap = jnp.minimum(cum_col[low] - v, 126.0)
                lows.append((scm[low, :] * jnp.exp2(gap)).astype(BF16))
            inner_top = dot(
                jnp.concatenate(tops, axis=1), jnp.concatenate([side[top] for side in sides], axis=0)
            )
            inner_low = dot(jnp.concatenate(lows, axis=1), jnp.concatenate(sides, axis=0))
            answer = jnp.concatenate([inner_top, inner_low], axis=0) + vecs[1:2, lanes] * value.astype(F32)
            carried = dot(cs[here], enter_q[b, :, lanes])
            local[here, lanes] = answer + dot(keepb[b], expand_a[:, lanes]) * carried
            keepx[here, lanes] = dot(colb[here], expand_b[:, lanes])
        return carry

    def answer(part):
        def scan(k, value):
            s_out[part, k, 0:share] = value.astype(BF16)
            tags = p_recv[part, k, share:].astype(F32)[0:8]
            decay = tags[0:1] + tags[1:2] + tags[2:3]
            return decay * value + p_recv[part, k, 0:share].astype(F32)

        every(lambda step, to: p_copy(part, step, me).wait_recv())
        final = lax.fori_loop(0, seq, scan, jnp.zeros((share, TILE), F32), unroll=8)
        even = lax.rem(me, 2) == 0
        zero = jnp.zeros_like(final)
        final = jnp.concatenate([jnp.where(even, final, zero), jnp.where(even, zero, final)], axis=0)
        asked = p_recv[part, :, share:].reshape(seq * HALO, TILE)
        replies = sum(dot(asked, piece.astype(BF16)) for piece in split3(final)[:2]).reshape(seq, HALO, TILE)[:, 8:]
        high = replies.astype(BF16).astype(F32)
        s_out[part, :, share:] = jnp.concatenate([high, replies - high], axis=1).astype(BF16)
        every(lambda step, to: s_copy(part, step, to).start())
        s_in[part, me] = s_out[part, me]

    lax.fori_loop(0, 1, block_local, 0)
    given_tokens()
    lax.fori_loop(1, blocks - 1, block_local, 0)
    answer(0)
    answer(1)
    lax.fori_loop(blocks - 1, blocks, block_local, 0)

    def carried_part(i, part):
        here = pl.ds(pl.multiple_of(i * TILE, TILE), TILE)
        readout = cs[here]
        pieces = []
        for g in range(pairs // 4):
            entering = jnp.concatenate(
                [
                    jnp.concatenate([s_in[part, 8 * g + 4 * p + t, 0:share] for t in range(4)], axis=0)
                    for p in range(2)
                ],
                axis=1,
            )
            at = part * inner // 2 + g * BLOCK
            lanes = slice(at, at + BLOCK)
            pieces.append(local[here, lanes] + keepx[here, lanes] * dot(readout, entering))
        squares = sum(piece * piece for piece in pieces)
        return here, pieces, squares[:, :TILE] + squares[:, TILE:]

    def finish_first(i, carry):
        here, pieces, squares = carried_part(i, 0)
        for g, piece in enumerate(pieces):
            local[here, g * BLOCK : (g + 1) * BLOCK] = piece
        colf[here] = squares
        return carry

    def finish(i, carry):
        here, pieces, squares = carried_part(i, 1)
        squares = jnp.sum(squares + colf[here], axis=1, keepdims=True)
        scale = lax.rsqrt(squares / inner + EPSILON)
        for g in range(pairs // 2):
            lanes = slice(g * BLOCK, (g + 1) * BLOCK)
            piece = local[here, lanes] if g < pairs // 4 else pieces[g - pairs // 4]
            obuf[here, lanes] = (piece * scale * gain[:, lanes]).astype(BF16)
        pltpu.make_async_copy(obuf.at[here], out.at[here], out_sem.at[i]).start()
        return carry

    every(lambda step, to: s_copy(0, step, to).wait_recv())
    lax.fori_loop(0, rows // TILE, finish_first, 0, unroll=2)
    every(lambda step, to: s_copy(1, step, to).wait_recv())
    lax.fori_loop(0, rows // TILE, finish, 0, unroll=2)

    def norm(pieces):
        squares = sum(piece * piece for piece in pieces)
        scale = lax.rsqrt(jnp.sum(squares, axis=1, keepdims=True) / inner + EPSILON)
        return [piece * scale for piece in pieces]

    pieces = []
    for p in range(pairs):
        lanes = slice(p * TILE, (p + 1) * TILE)
        part, first = 2 * p // pairs, 4 * p % seq
        tags = sum(s_in[part, first + t, share:].astype(F32) for t in range(4))
        pieces.append(dec_local[:, lanes] + dec_keep[:, lanes] * (tags[0:8] + tags[8:16]))
    for p, piece in enumerate(norm(pieces)):
        lanes = slice(p * TILE, (p + 1) * TILE)
        dec_out[:, lanes] = (piece * gain[:, lanes]).astype(BF16)

    @pl.when(me < last)
    def _():
        rim_copy(me + 1).wait_send()

    @pl.when(me == last)
    def _():
        def sent(to, carry):
            tail_copy(to).wait_send()
            return carry

        lax.fori_loop(0, last, sent, 0)

    def settle(step, to):
        for copy in (p_copy, s_copy):
            for part in range(2):
                copy(part, step, to).wait_send()

    every(settle)

    def written(i, carry):
        here = pl.ds(pl.multiple_of(i * TILE, TILE), TILE)
        pltpu.make_async_copy(obuf.at[here], out.at[here], out_sem.at[i]).wait()
        return carry

    lax.fori_loop(0, rows // TILE, written, 0)


def hand_over(held, held_dec, out, out_dec, buf, buf_dec, sem):
    rows = held.shape[0]
    count = sem.shape[1] - 1
    pairs = [((held_dec, buf_dec), (buf_dec, out_dec))]
    for i in range(count):
        here = pl.ds(i * rows // count, rows // count)
        pairs.append(((held.at[here], buf.at[here]), (buf.at[here], out.at[here])))
    copies = [
        [pltpu.make_async_copy(*move, sem.at[way, i]) for way, move in enumerate(moves)]
        for i, moves in enumerate(pairs)
    ]
    for come, _ in copies:
        come.start()
    for come, go in copies:
        come.wait()
        go.start()
    for _, go in copies:
        go.wait()


def body(
    x_in, bc_in, dt_in, conv_x, conv_bc, a_log, dt_bias, d_skip, norm_gain, doc_lengths, dec_x, dec_bc, dec_dt
):
    rows, inner = x_in.shape
    heads = dt_in.shape[1]
    double = bc_in.shape[2]
    state = double // 2
    seq = lax.axis_size("seq")
    blocks = rows // BLOCK
    edge_rows = 4 * (inner + double) // TILE
    whole = pl.BlockSpec(memory_space=pl.ANY)
    near = pl.BlockSpec(memory_space=pltpu.VMEM)
    dma = pltpu.SemaphoreType.DMA
    vmem = pltpu.VMEM
    prompt, decoded = pl.pallas_call(
        functools.partial(kernel, seq),
        out_shape=(
            jax.ShapeDtypeStruct((rows, inner), BF16),
            jax.ShapeDtypeStruct((8, inner), BF16),
        ),
        in_specs=[whole] * 13,
        out_specs=(whole, near),
        scratch_shapes=[
            vmem(conv_x.shape, F32),
            vmem(conv_bc.shape, F32),
            vmem((1, heads), F32),
            vmem((1, heads), F32),
            vmem((1, heads), F32),
            vmem((1, inner), F32),
            pltpu.SMEM(doc_lengths.shape, jnp.int32),
            vmem((8, inner), BF16),
            vmem((8, double), BF16),
            vmem((8, heads), F32),
            vmem((HALO + rows, inner), BF16),
            vmem((HALO + rows, double), BF16),
            vmem((heads, rows), F32),
            vmem((edge_rows, TILE), BF16),
            vmem((edge_rows, TILE), BF16),
            vmem((edge_rows, TILE), BF16),
            vmem((2 * edge_rows, TILE), F32),
            vmem((rows, inner), BF16),
            vmem((rows, inner), BF16),
            vmem((rows, state), BF16),
            vmem((rows, state), BF16),
            vmem((state, rows), BF16),
            vmem((TILE, inner), BF16),
            vmem((TILE, inner), BF16),
            vmem((rows, TILE), F32),
            vmem((rows, TILE), BF16),
            vmem((blocks, BLOCK, TILE), BF16),
            vmem((blocks, heads, BLOCK), F32),
            vmem((8, inner), F32),
            vmem((blocks, state, inner), BF16),
            vmem((2, seq, state // 4 + HALO, TILE), BF16),
            vmem((2, seq, state // 4 + HALO, TILE), BF16),
            vmem((2, seq, state // 4 + HALO, TILE), BF16),
            vmem((2, seq, state // 4 + HALO, TILE), BF16),
            vmem((rows, inner), F32),
            vmem((rows, inner), F32),
            vmem((BLOCK, BLOCK), F32),
            vmem((TILE, TILE), F32),
            vmem((8, inner), F32),
            vmem((72, TILE), BF16),
            vmem((rows, inner), BF16),
            vmem((8, inner), F32),
            vmem((8, inner), F32),
            dma((11,)),
            dma((2 * blocks,)),
            dma((1,)),
            dma((1,)),
            dma((seq,)),
            dma((1,)),
        ]
        + [dma((2, seq))] * 4
        + [dma((rows // TILE,))],
        compiler_params=pltpu.CompilerParams(
            collective_id=0, has_side_effects=True, vmem_limit_bytes=60 << 20
        ),
    )(
        x_in,
        bc_in.reshape(rows, double),
        dt_in.T,
        conv_x,
        conv_bc,
        a_log.reshape(1, heads),
        dt_bias.reshape(1, heads),
        d_skip.reshape(1, heads),
        norm_gain.reshape(1, inner),
        doc_lengths,
        dec_x.reshape(8, inner),
        dec_bc.reshape(8, double),
        dec_dt.reshape(8, heads),
    )
    prompt, decoded = pl.pallas_call(
        hand_over,
        out_shape=(
            jax.ShapeDtypeStruct((rows, inner), BF16),
            jax.ShapeDtypeStruct((8, inner), BF16),
        ),
        in_specs=[whole] * 2,
        out_specs=(whole, whole),
        scratch_shapes=[vmem((rows, inner), BF16), vmem((8, inner), BF16), dma((2, 7))],
        compiler_params=pltpu.CompilerParams(vmem_limit_bytes=60 << 20),
    )(prompt, decoded)
    return prompt, decoded.reshape(1, 8, inner)


def solution(mesh):
    placed = (
        P(("group", "seq"), "head"),
        P(("group", "seq"), "head", None),
        P(("group", "seq"), "head"),
        P(None, "head"),
        P(None, "head", None),
        P("head"),
        P("head"),
        P("head"),
        P("head"),
        P("group"),
        P(("group", "seq"), None, "head"),
        P(("group", "seq"), None, "head", None),
        P(("group", "seq"), None, "head"),
    )
    return jax.shard_map(
        body,
        mesh=mesh,
        in_specs=placed,
        out_specs=(P(("group", "seq"), "head"), P(("group", "seq"), None, "head")),
        check_vma=False,
    )
```

time: 39.5 us -> 34.6 us (0.88)
  local copies, waits for them, and re-layouts: 3.28 us -> 0 us
  Pallas kernels: 35.5 us -> 33.7 us
    pallas_call x1, Pallas kernels: 35.5 us -> 31.5 us  [body(): pl.pallas_call(functools.partial(kernel, seq), out_shape=(jax.ShapeDtypeS...]
    unnamed x4 -> x0, local copies, waits for them, and re-layouts: 3.28 us -> none
    pallas_call x0 -> x1, Pallas kernels: none -> 2.22 us  [body(): pl.pallas_call(hand_over, out_shape=(jax.ShapeDtypeStruct((rows, inner),...]
where the time goes in v2:
time: 34.6 us; the launch traced here: 34.4 us
  Pallas kernels  33.7 us (97%)
  between operations  0.64 us (2%)
    pallas_call x1, Pallas kernels, body(): pl.pallas_call(functools.partial(kernel, seq), out_shape=(jax.ShapeDtypeS...  31.5 us
    pallas_call x1, Pallas kernels, body(): pl.pallas_call(hand_over, out_shape=(jax.ShapeDtypeStruct((rows, inner),...  2.22 us

profile of v2, /device:TPU:32, one launch (start us, length us, event | category | flops | bytes accessed | tf_op | source)
XLA Modules:
  0.0 34.4 jit_solution(5722370720460273015)
XLA Ops:
  0.6 31.5 %shard_map.140 = (bf16[768,1024]{1,0:T(8,128)(2,1)}, bf16[8,1024]{1,0:T(8,128)(2,1)}) custom-call(bf16[768,1024]{1,0:T(8,128)(2,1)} %x_hbm.1, bf16[768,512]{1,0:T(8,128)(2,1)} %bitcast.10, f32[16,768]{1,0:T(8,128)} %bitcast.11, f32[4,1024]{1,0:T(4,128)} %conv_x_hbm.1, f32[4,1,512]{2,1,0:T(1,128)} %conv_bc_hbm.1, f32[1,16]{1,0:T(1,128)} %bitcast.16, ...), custom_call_target="tpu_custom_call" | custom-call | tf_op jit(solution)/shard_map/pallas_call | solution.py:596
  32.1 2.2 %shard_map.141 = (bf16[768,1024]{1,0:T(8,128)(2,1)}, bf16[8,1024]{1,0:T(8,128)(2,1)}) custom-call(bf16[768,1024]{1,0:T(8,128)(2,1)} %get-tuple-element.6.held, bf16[8,1024]{1,0:T(8,128)(2,1)} %get-tuple-element.7.held_dec), custom_call_target="tpu_custom_call" | custom-call | tf_op jit(solution)/shard_map/pallas_call | solution.py:675

commit v3 on v2

--- a/solution.py
+++ b/solution.py
@@ -52,9 +52,9 @@
     out, dec_out,
     conv_x, conv_bc, a_log, dt_bias, d_skip, gain, doc, dec_x, dec_bc, dec_dt,
     xbuf, bcbuf, dtbuf, rim_msg, rim_recv, tail_recv, tail_f32, xs, xw, bs, cs, bst, expand_a, expand_b, colf, colb, keepb,
-    vrow, vecs, enter_q, p_msg, p_recv, s_out, s_in,
-    local, keepx, scm, small, edges, dec_factors, obuf, dec_keep, dec_local,
-    few_sem, load_sem, rim_ss, rim_rs, tail_ss, tail_rs, p_ss, p_rs, s_ss, s_rs, out_sem,
+    vrow, vecs, enter_q, p_msg, p_recv, s_out, s_in, d_msg, d_recv, c_msg, c_recv, y_msg, y_recv,
+    local, keepx, scm, small, dec_factors, obuf, dec_keep, dec_local,
+    few_sem, load_sem, rim_ss, rim_rs, tail_ss, tail_rs, p_ss, p_rs, s_ss, s_rs, d_ss, d_rs, c_ss, c_rs, y_ss, y_rs, out_sem,
 ):
     me = lax.axis_index("seq")
     rows, inner = xs.shape
@@ -84,7 +84,7 @@
         (dec_dt_hbm, dec_dt),
     ]
     few = [pltpu.make_async_copy(far, near, few_sem.at[i]) for i, (far, near) in enumerate(few)]
-    for copy in few:
+    for copy in few[:5]:
         copy.start()
     loads = []
     for b in reversed(range(blocks)):
@@ -95,8 +95,9 @@
                 pltpu.make_async_copy(bc_hbm.at[there], bcbuf.at[here], load_sem.at[2 * b + 1]),
             )
         )
-        for copy in loads[-1]:
-            copy.start()
+
+    for copy in loads[0]:
+        copy.start()
 
     barrier = pltpu.get_barrier_semaphore()
 
@@ -105,6 +106,12 @@
         return carry
 
     lax.fori_loop(1, seq, greet, 0)
+
+    for copy in few[5:]:
+        copy.start()
+    for pair in loads[1:]:
+        for copy in pair:
+            copy.start()
 
     few[0].wait()
     ends = []
@@ -202,6 +209,11 @@
     picked = jnp.concatenate(split3(picked) + [jnp.zeros((TILE - 3 * heads, TILE), F32)], axis=0)
     vecs[...] = dot(picked.T.astype(BF16), expand_a[...])[0:8]
 
+    first_row = lax.broadcasted_iota(jnp.int32, (8, TILE), 0) == 0
+    for to in range(seq):
+        sides = [vecs[0:1, at : at + TILE] for at in (to // 4 * TILE, to // 4 * TILE + inner // 2)]
+        d_msg[to] = jnp.where(first_row, sides[0], sides[1])
+
     for copy in few[5:]:
         copy.wait()
     for copy in loads[0]:
@@ -242,6 +254,46 @@
     @pl.when(me == 0)
     def _():
         rim_recv[...] = jnp.zeros_like(rim_recv)
+
+    def p_copy(part, step, to):
+        return pltpu.make_async_remote_copy(
+            src_ref=p_msg.at[part, to], dst_ref=p_recv.at[part, me], send_sem=p_ss.at[part, step],
+            recv_sem=p_rs.at[part, step], device_id={"seq": to}, device_id_type=MESH,
+        )
+
+    def s_copy(part, step, to):
+        return pltpu.make_async_remote_copy(
+            src_ref=s_out.at[part, to], dst_ref=s_in.at[part, me], send_sem=s_ss.at[part, step],
+            recv_sem=s_rs.at[part, step], device_id={"seq": to}, device_id_type=MESH,
+        )
+
+    def d_copy(step, to):
+        return pltpu.make_async_remote_copy(
+            src_ref=d_msg.at[to], dst_ref=d_recv.at[me], send_sem=d_ss.at[step],
+            recv_sem=d_rs.at[step], device_id={"seq": to}, device_id_type=MESH,
+        )
+
+    def c_copy(step, to):
+        return pltpu.make_async_remote_copy(
+            src_ref=c_msg.at[lax.rem(lax.div(to, 2), 2)], dst_ref=c_recv.at[me], send_sem=c_ss.at[step],
+            recv_sem=c_rs.at[step], device_id={"seq": to}, device_id_type=MESH,
+        )
+
+    def y_copy(step, to):
+        return pltpu.make_async_remote_copy(
+            src_ref=y_msg.at[to], dst_ref=y_recv.at[me], send_sem=y_ss.at[step],
+            recv_sem=y_rs.at[step], device_id={"seq": to}, device_id_type=MESH,
+        )
+
+    def every(action):
+        def body(step, carry):
+            action(step, peer(step))
+            return carry
+
+        lax.fori_loop(1, seq, body, 0)
+
+    every(lambda step, to: d_copy(step, to).start())
+    d_recv[me] = d_msg[me]
 
     def linked_rows(row):
         positions = base + row - 8 + lax.broadcasted_iota(jnp.int32, (TILE + 8, TILE), 0)
@@ -300,51 +352,6 @@
             copy.wait()
     lax.fori_loop(0, rows // TILE, conv_rows, 0, unroll=2)
 
-    offsets = lax.broadcasted_iota(jnp.int32, (16, TILE), 0)
-    tail_doc = jnp.int32(0)
-    for end in ends:
-        tail_doc = tail_doc + (end <= total_rows - 1).astype(jnp.int32)
-    joined = (tail_doc == docs - 1).astype(F32)
-    dec_linked = jnp.where(
-        offsets < 8, linked_of(total_rows - 8 + offsets), jnp.where(offsets == 8, joined, 1.0)
-    )
-
-    def dec_conv(tail_at, given, taps, at):
-        lanes = pl.ds(at, TILE)
-        ext = jnp.concatenate([tail_f32[pl.ds(tail_at, 8)], given[:, lanes].astype(F32)], axis=0)
-        return silu(conv_chain(ext, [tap(lanes) for tap in taps], dec_linked)[8:]).astype(BF16).astype(F32)
-
-    @pl.when(me != last)
-    def _():
-        tail_copy(me).wait_recv()
-
-    tail = tail_recv[...].astype(F32)
-    spaced = []
-    for t in range(tail.shape[0] // 4):
-        spaced += [jnp.zeros((4, TILE), F32), tail[4 * t : 4 * t + 4]]
-    tail_f32[...] = jnp.concatenate(spaced, axis=0)
-    dec_bcs = [dec_conv(8 * (pairs + at // TILE), dec_bc, bc_taps, at) for at in range(0, 2 * state, TILE)]
-
-    def p_copy(part, step, to):
-        return pltpu.make_async_remote_copy(
-            src_ref=p_msg.at[part, to], dst_ref=p_recv.at[part, me], send_sem=p_ss.at[part, step],
-            recv_sem=p_rs.at[part, step], device_id={"seq": to}, device_id_type=MESH,
-        )
-
-    def s_copy(part, step, to):
-        return pltpu.make_async_remote_copy(
-            src_ref=s_out.at[part, to], dst_ref=s_in.at[part, me], send_sem=s_ss.at[part, step],
-            recv_sem=s_rs.at[part, step], device_id={"seq": to}, device_id_type=MESH,
-        )
-
-    def every(action):
-        def body(step, carry):
-            action(step, peer(step))
-            return carry
-
-        lax.fori_loop(1, seq, body, 0)
-
-    edges[...] = jnp.concatenate(split3(vecs[0:1, :]) + [jnp.zeros((5, inner), F32)], axis=0)
     enter_q[0] = jnp.zeros((state, inner), BF16)
     share = state // 4
 
@@ -358,11 +365,9 @@
                 value = vecs[2 + b : 3 + b, lanes] * value + dot(bst[:, here], xw[here, lanes])
             value = value.astype(BF16)
             for p in range(2):
-                decay = edges[:, g * BLOCK + p * TILE : g * BLOCK + (p + 1) * TILE]
                 for quarter in range(4):
                     to = (8 * g + 4 * p + quarter) % seq
-                    p_msg[part, to, 0:share] = value[quarter * share : (quarter + 1) * share, p * TILE : (p + 1) * TILE]
-                    p_msg[part, to, share:] = jnp.concatenate([decay, dec_bcs[2 + quarter // 2]], axis=0).astype(BF16)
+                    p_msg[part, to] = value[quarter * share : (quarter + 1) * share, p * TILE : (p + 1) * TILE]
 
                     @pl.when(to != me)
                     def _(to=to):
@@ -373,6 +378,36 @@
     contribute(0)
     contribute(1)
     lax.fori_loop(0, rows // TILE, conv_c_rows, 0, unroll=2)
+
+    offsets = lax.broadcasted_iota(jnp.int32, (16, TILE), 0)
+    tail_doc = jnp.int32(0)
+    for end in ends:
+        tail_doc = tail_doc + (end <= total_rows - 1).astype(jnp.int32)
+    joined = (tail_doc == docs - 1).astype(F32)
+    dec_linked = jnp.where(
+        offsets < 8, linked_of(total_rows - 8 + offsets), jnp.where(offsets == 8, joined, 1.0)
+    )
+
+    def dec_conv(tail_at, given, taps, at):
+        lanes = pl.ds(at, TILE)
+        ext = jnp.concatenate([tail_f32[pl.ds(tail_at, 8)], given[:, lanes].astype(F32)], axis=0)
+        return silu(conv_chain(ext, [tap(lanes) for tap in taps], dec_linked)[8:]).astype(BF16).astype(F32)
+
+    @pl.when(me != last)
+    def _():
+        tail_copy(me).wait_recv()
+
+    tail = tail_recv[...].astype(F32)
+    spaced = []
+    for t in range(tail.shape[0] // 4):
+        spaced += [jnp.zeros((4, TILE), F32), tail[4 * t : 4 * t + 4]]
+    tail_f32[...] = jnp.concatenate(spaced, axis=0)
+    dec_bcs = [dec_conv(8 * (pairs + at // TILE), dec_bc, bc_taps, at) for at in range(0, 2 * state, TILE)]
+
+    for i in range(2):
+        c_msg[i] = jnp.concatenate([dec_bcs[2 + i], jnp.zeros((8, TILE), F32)], axis=0).astype(BF16)
+    every(lambda step, to: c_copy(step, to).start())
+    c_recv[me] = c_msg[lax.rem(lax.div(me, 2), 2)]
 
     def lane_dot(a, b):
         return lax.dot_general(a, b, (((1,), (1,)), ((), ())), preferred_element_type=F32)
@@ -452,28 +487,33 @@
 
     def answer(part):
         def scan(k, value):
-            s_out[part, k, 0:share] = value.astype(BF16)
-            tags = p_recv[part, k, share:].astype(F32)[0:8]
-            decay = tags[0:1] + tags[1:2] + tags[2:3]
-            return decay * value + p_recv[part, k, 0:share].astype(F32)
+            s_out[part, k] = value.astype(BF16)
+            return d_recv[k, part : part + 1] * value + p_recv[part, k].astype(F32)
 
         every(lambda step, to: p_copy(part, step, me).wait_recv())
         final = lax.fori_loop(0, seq, scan, jnp.zeros((share, TILE), F32), unroll=8)
+        every(lambda step, to: s_copy(part, step, to).start())
+        s_in[part, me] = s_out[part, me]
+        return final
+
+    def reply(part, final):
         even = lax.rem(me, 2) == 0
         zero = jnp.zeros_like(final)
         final = jnp.concatenate([jnp.where(even, final, zero), jnp.where(even, zero, final)], axis=0)
-        asked = p_recv[part, :, share:].reshape(seq * HALO, TILE)
-        replies = sum(dot(asked, piece.astype(BF16)) for piece in split3(final)[:2]).reshape(seq, HALO, TILE)[:, 8:]
-        high = replies.astype(BF16).astype(F32)
-        s_out[part, :, share:] = jnp.concatenate([high, replies - high], axis=1).astype(BF16)
-        every(lambda step, to: s_copy(part, step, to).start())
-        s_in[part, me] = s_out[part, me]
+        asked = c_recv[...].reshape(seq * HALO, TILE)
+        replies = sum(dot(asked, piece.astype(BF16)) for piece in split3(final)).reshape(seq, HALO, TILE)
+        y_msg[:, 8 * part : 8 * part + 8] = replies[:, 0:8]
 
     lax.fori_loop(0, 1, block_local, 0)
     given_tokens()
     lax.fori_loop(1, blocks - 1, block_local, 0)
-    answer(0)
-    answer(1)
+    every(lambda step, to: d_copy(step, to).wait_recv())
+    finals = [answer(0), answer(1)]
+    every(lambda step, to: c_copy(step, to).wait_recv())
+    for part, final in enumerate(finals):
+        reply(part, final)
+    every(lambda step, to: y_copy(step, to).start())
+    y_recv[me] = y_msg[me]
     lax.fori_loop(blocks - 1, blocks, block_local, 0)
 
     def carried_part(i, part):
@@ -483,7 +523,7 @@
         for g in range(pairs // 4):
             entering = jnp.concatenate(
                 [
-                    jnp.concatenate([s_in[part, 8 * g + 4 * p + t, 0:share] for t in range(4)], axis=0)
+                    jnp.concatenate([s_in[part, 8 * g + 4 * p + t] for t in range(4)], axis=0)
                     for p in range(2)
                 ],
                 axis=1,
@@ -517,6 +557,7 @@
     every(lambda step, to: s_copy(1, step, to).wait_recv())
     lax.fori_loop(0, rows // TILE, finish, 0, unroll=2)
 
+    every(lambda step, to: y_copy(step, to).wait_recv())
     def norm(pieces):
         squares = sum(piece * piece for piece in pieces)
         scale = lax.rsqrt(jnp.sum(squares, axis=1, keepdims=True) / inner + EPSILON)
@@ -526,8 +567,8 @@
     for p in range(pairs):
         lanes = slice(p * TILE, (p + 1) * TILE)
         part, first = 2 * p // pairs, 4 * p % seq
-        tags = sum(s_in[part, first + t, share:].astype(F32) for t in range(4))
-        pieces.append(dec_local[:, lanes] + dec_keep[:, lanes] * (tags[0:8] + tags[8:16]))
+        reading = sum(y_recv[first + t, 8 * part : 8 * part + 8] for t in range(4))
+        pieces.append(dec_local[:, lanes] + dec_keep[:, lanes] * reading)
     for p, piece in enumerate(norm(pieces)):
         lanes = slice(p * TILE, (p + 1) * TILE)
         dec_out[:, lanes] = (piece * gain[:, lanes]).astype(BF16)
@@ -548,6 +589,8 @@
         for copy in (p_copy, s_copy):
             for part in range(2):
                 copy(part, step, to).wait_send()
+        for copy in (d_copy, c_copy, y_copy):
+            copy(step, to).wait_send()
 
     every(settle)
 
@@ -632,15 +675,20 @@
             vmem((blocks, heads, BLOCK), F32),
             vmem((8, inner), F32),
             vmem((blocks, state, inner), BF16),
-            vmem((2, seq, state // 4 + HALO, TILE), BF16),
-            vmem((2, seq, state // 4 + HALO, TILE), BF16),
-            vmem((2, seq, state // 4 + HALO, TILE), BF16),
-            vmem((2, seq, state // 4 + HALO, TILE), BF16),
+            vmem((2, seq, state // 4, TILE), BF16),
+            vmem((2, seq, state // 4, TILE), BF16),
+            vmem((2, seq, state // 4, TILE), BF16),
+            vmem((2, seq, state // 4, TILE), BF16),
+            vmem((seq, 8, TILE), F32),
+            vmem((seq, 8, TILE), F32),
+            vmem((2, HALO, TILE), BF16),
+            vmem((seq, HALO, TILE), BF16),
+            vmem((seq, 16, TILE), F32),
+            vmem((seq, 16, TILE), F32),
             vmem((rows, inner), F32),
             vmem((rows, inner), F32),
             vmem((BLOCK, BLOCK), F32),
             vmem((TILE, TILE), F32),
-            vmem((8, inner), F32),
             vmem((72, TILE), BF16),
             vmem((rows, inner), BF16),
             vmem((8, inner), F32),
@@ -653,6 +701,7 @@
             dma((1,)),
         ]
         + [dma((2, seq))] * 4
+        + [dma((seq,))] * 6
         + [dma((rows // TILE,))],
         compiler_params=pltpu.CompilerParams(
             collective_id=0, has_side_effects=True, vmem_limit_bytes=60 << 20

time: 34.6 us -> 34.3 us (level)
  no operation moved by 1% of the time
where the time goes in v3:
time: 34.3 us; the launch traced here: 34.1 us
  Pallas kernels  33.5 us (98%)
  between operations  0.64 us (2%)
    pallas_call x1, Pallas kernels, body(): pl.pallas_call(functools.partial(kernel, seq), out_shape=(jax.ShapeDtypeS...  31.2 us
    pallas_call x1, Pallas kernels, body(): pl.pallas_call(hand_over, out_shape=(jax.ShapeDtypeStruct((rows, inner),...  2.22 us

profile of v3, /device:TPU:32, one launch (start us, length us, event | category | flops | bytes accessed | tf_op | source)
XLA Modules:
  0.0 34.1 jit_solution(294776845514445865)
XLA Ops:
  0.6 31.2 %shard_map.140 = (bf16[768,1024]{1,0:T(8,128)(2,1)}, bf16[8,1024]{1,0:T(8,128)(2,1)}) custom-call(bf16[768,1024]{1,0:T(8,128)(2,1)} %x_hbm.1, bf16[768,512]{1,0:T(8,128)(2,1)} %bitcast.10, f32[16,768]{1,0:T(8,128)} %bitcast.11, f32[4,1024]{1,0:T(4,128)} %conv_x_hbm.1, f32[4,1,512]{2,1,0:T(1,128)} %conv_bc_hbm.1, f32[1,16]{1,0:T(1,128)} %bitcast.16, ...), custom_call_target="tpu_custom_call" | custom-call | tf_op jit(solution)/shard_map/pallas_call | solution.py:639
  31.9 2.2 %shard_map.141 = (bf16[768,1024]{1,0:T(8,128)(2,1)}, bf16[8,1024]{1,0:T(8,128)(2,1)}) custom-call(bf16[768,1024]{1,0:T(8,128)(2,1)} %get-tuple-element.6.held, bf16[8,1024]{1,0:T(8,128)(2,1)} %get-tuple-element.7.held_dec), custom_call_target="tpu_custom_call" | custom-call | tf_op jit(solution)/shard_map/pallas_call | solution.py:724

commit v4 on v3

--- a/solution.py
+++ b/solution.py
@@ -53,7 +53,7 @@
     conv_x, conv_bc, a_log, dt_bias, d_skip, gain, doc, dec_x, dec_bc, dec_dt,
     xbuf, bcbuf, dtbuf, rim_msg, rim_recv, tail_recv, tail_f32, xs, xw, bs, cs, bst, expand_a, expand_b, colf, colb, keepb,
     vrow, vecs, enter_q, p_msg, p_recv, s_out, s_in, d_msg, d_recv, c_msg, c_recv, y_msg, y_recv,
-    local, keepx, scm, small, dec_factors, obuf, dec_keep, dec_local,
+    local, keepx, scm, small, dec_factors, shifted, obuf, dec_buf, dec_keep, dec_local,
     few_sem, load_sem, rim_ss, rim_rs, tail_ss, tail_rs, p_ss, p_rs, s_ss, s_rs, d_ss, d_rs, c_ss, c_rs, y_ss, y_rs, out_sem,
 ):
     me = lax.axis_index("seq")
@@ -297,12 +297,20 @@
 
     def linked_rows(row):
         positions = base + row - 8 + lax.broadcasted_iota(jnp.int32, (TILE + 8, TILE), 0)
-        return linked_of(positions)
+        one = linked_of(positions)
+        two = one * pltpu.roll(one, 1, 0)
+        three = one * pltpu.roll(two, 1, 0)
+        return [same[8:] for same in (one, two, three)]
 
     def conv_tile(buf, taps, row, at, linked):
         lanes = slice(at, at + TILE)
+        slot = shifted.at[at // TILE + (pairs if buf is bcbuf else 0)]
         raw = buf[pl.ds(row, TILE + HALO), lanes].astype(F32)[HALO - 8 :]
-        return silu(conv_chain(raw, [tap(lanes) for tap in taps], linked)[8:]).astype(BF16)
+        slot[...] = raw
+        total = taps[3](lanes) * raw[8:]
+        for back, same in enumerate(linked, 1):
+            total = total + taps[3 - back](lanes) * slot[8 - back : 8 - back + TILE] * same
+        return silu(total).astype(BF16)
 
     x_taps = [lambda lanes, k=k: conv_x[k : k + 1, lanes] for k in range(4)]
     bc_taps = [lambda lanes, k=k: conv_bc[k, :, lanes] for k in range(4)]
@@ -552,10 +560,31 @@
         pltpu.make_async_copy(obuf.at[here], out.at[here], out_sem.at[i]).start()
         return carry
 
+    @pl.when(me < last)
+    def _():
+        rim_copy(me + 1).wait_send()
+
+    @pl.when(me == last)
+    def _():
+        def sent(to, carry):
+            tail_copy(to).wait_send()
+            return carry
+
+        lax.fori_loop(0, last, sent, 0)
+
+    def settle(step, to):
+        for copy in (p_copy, s_copy):
+            for part in range(2):
+                copy(part, step, to).wait_send()
+        for copy in (d_copy, c_copy, y_copy):
+            copy(step, to).wait_send()
+
+    every(settle)
+
     every(lambda step, to: s_copy(0, step, to).wait_recv())
     lax.fori_loop(0, rows // TILE, finish_first, 0, unroll=2)
     every(lambda step, to: s_copy(1, step, to).wait_recv())
-    lax.fori_loop(0, rows // TILE, finish, 0, unroll=2)
+    lax.fori_loop(0, rows // TILE - 2, finish, 0, unroll=2)
 
     every(lambda step, to: y_copy(step, to).wait_recv())
     def norm(pieces):
@@ -571,28 +600,12 @@
         pieces.append(dec_local[:, lanes] + dec_keep[:, lanes] * reading)
     for p, piece in enumerate(norm(pieces)):
         lanes = slice(p * TILE, (p + 1) * TILE)
-        dec_out[:, lanes] = (piece * gain[:, lanes]).astype(BF16)
-
-    @pl.when(me < last)
-    def _():
-        rim_copy(me + 1).wait_send()
-
-    @pl.when(me == last)
-    def _():
-        def sent(to, carry):
-            tail_copy(to).wait_send()
-            return carry
-
-        lax.fori_loop(0, last, sent, 0)
-
-    def settle(step, to):
-        for copy in (p_copy, s_copy):
-            for part in range(2):
-                copy(part, step, to).wait_send()
-        for copy in (d_copy, c_copy, y_copy):
-            copy(step, to).wait_send()
-
-    every(settle)
+        dec_buf[:, lanes] = (piece * gain[:, lanes]).astype(BF16)
+    dec_done = pltpu.make_async_copy(dec_buf, dec_out, out_sem.at[rows // TILE])
+    dec_done.start()
+
+    lax.fori_loop(rows // TILE - 2, rows // TILE, finish, 0, unroll=2)
+
 
     def written(i, carry):
         here = pl.ds(pl.multiple_of(i * TILE, TILE), TILE)
@@ -600,6 +613,7 @@
         return carry
 
     lax.fori_loop(0, rows // TILE, written, 0)
+    dec_done.wait()
 
 
 def hand_over(held, held_dec, out, out_dec, buf, buf_dec, sem):
@@ -633,7 +647,6 @@
     blocks = rows // BLOCK
     edge_rows = 4 * (inner + double) // TILE
     whole = pl.BlockSpec(memory_space=pl.ANY)
-    near = pl.BlockSpec(memory_space=pltpu.VMEM)
     dma = pltpu.SemaphoreType.DMA
     vmem = pltpu.VMEM
     prompt, decoded = pl.pallas_call(
@@ -643,7 +656,7 @@
             jax.ShapeDtypeStruct((8, inner), BF16),
         ),
         in_specs=[whole] * 13,
-        out_specs=(whole, near),
+        out_specs=(whole, whole),
         scratch_shapes=[
             vmem(conv_x.shape, F32),
             vmem(conv_bc.shape, F32),
@@ -690,7 +703,9 @@
             vmem((BLOCK, BLOCK), F32),
             vmem((TILE, TILE), F32),
             vmem((72, TILE), BF16),
+            vmem(((inner + double) // TILE, TILE + 8, TILE), F32),
             vmem((rows, inner), BF16),
+            vmem((8, inner), BF16),
             vmem((8, inner), F32),
             vmem((8, inner), F32),
             dma((11,)),
@@ -702,7 +717,7 @@
         ]
         + [dma((2, seq))] * 4
         + [dma((seq,))] * 6
-        + [dma((rows // TILE,))],
+        + [dma((rows // TILE + 1,))],
         compiler_params=pltpu.CompilerParams(
             collective_id=0, has_side_effects=True, vmem_limit_bytes=60 << 20
         ),

time: 34.3 us -> 33.5 us (0.977)
  Pallas kernels: 33.5 us -> 32.7 us
    pallas_call x1, Pallas kernels: 31.2 us -> 30.5 us  [body(): pl.pallas_call(functools.partial(kernel, seq), out_shape=(jax.ShapeDtypeS...]
where the time goes in v4:
time: 33.5 us; the launch traced here: 33.3 us
  Pallas kernels  32.7 us (98%)
  between operations  0.64 us (2%)
    pallas_call x1, Pallas kernels, body(): pl.pallas_call(functools.partial(kernel, seq), out_shape=(jax.ShapeDtypeS...  30.5 us
    pallas_call x1, Pallas kernels, body(): pl.pallas_call(hand_over, out_shape=(jax.ShapeDtypeStruct((rows, inner),...  2.22 us

profile of v4, /device:TPU:32, one launch (start us, length us, event | category | flops | bytes accessed | tf_op | source)
XLA Modules:
  0.0 33.3 jit_solution(6509261935527489857)
XLA Ops:
  0.6 30.5 %shard_map.140 = (bf16[768,1024]{1,0:T(8,128)(2,1)}, bf16[8,1024]{1,0:T(8,128)(2,1)}) custom-call(bf16[768,1024]{1,0:T(8,128)(2,1)} %x_hbm.1, bf16[768,512]{1,0:T(8,128)(2,1)} %bitcast.10, f32[16,768]{1,0:T(8,128)} %bitcast.11, f32[4,1024]{1,0:T(4,128)} %conv_x_hbm.1, f32[4,1,512]{2,1,0:T(1,128)} %conv_bc_hbm.1, f32[1,16]{1,0:T(1,128)} %bitcast.16, ...), custom_call_target="tpu_custom_call" | custom-call | tf_op jit(solution)/shard_map/pallas_call | solution.py:652
  31.1 2.2 %shard_map.141 = (bf16[768,1024]{1,0:T(8,128)(2,1)}, bf16[8,1024]{1,0:T(8,128)(2,1)}) custom-call(bf16[768,1024]{1,0:T(8,128)(2,1)} %get-tuple-element.6.held, bf16[8,1024]{1,0:T(8,128)(2,1)} %get-tuple-element.7.held_dec), custom_call_target="tpu_custom_call" | custom-call | tf_op jit(solution)/shard_map/pallas_call | solution.py:739
